TPU v7x, 256 devices: a whole 4x4x8 slice. The times are simulated.
256 devices in a mesh: ctx: 32 (over y, z), tp: 8 (over x, core).
Axes of the slice: x: 4, y: 4, z: 8, core: 2. Of those that a mesh axis runs over, the one named last changes fastest.
Arguments:
- queries: bfloat16 [2048, 8192], P('ctx', 'tp'), as said below
- new_keys: bfloat16 [2048, 1024], P('ctx', 'tp'), may hold values from -5 to 5
- new_values: bfloat16 [2048, 1024], P('ctx', 'tp'), may hold values from -5 to 5
- cache_keys: bfloat16 [8, 24576, 1024], P(None, 'ctx', 'tp'), as said below
- cache_values: bfloat16 [8, 24576, 1024], P(None, 'ctx', 'tp'), may hold values from -5 to 5
- cache_lengths: int32 [8, 32], P(None, 'ctx'), may hold values from 1 to 768, 12288 in all within a row
- turn_start: int32 [8], replicated, may hold values from 0 to 127
- out_weight: bfloat16 [8192, 4096], P('tp'), may hold values from -0.0625 to 0.0625
Outputs:
- mixed: bfloat16 [2048, 4096], P(('ctx', 'tp'))
Inputs may be any that keep to these rules, and one draw needn't show every extreme that they name: `queries`: within -8 to 8. `cache_keys`: within -8 to 8. `cache_lengths`: every shard holds one filled position at least; 768 is reached in every trajectory.
All inputs are finite; a program needn't handle non-finite values.
Results may differ from a plain program's by a relative error of at most 0.022.
Values may be sent and summed in bfloat16 or wider, within the bound.
A program may use at most 128 MiB of HBM per device.

v0:
```python
import math

import jax
import jax.numpy as jnp
from jax import lax
from jax.sharding import PartitionSpec as P

H = 64
KVH = 8
HD = 128
NEW = 256


masked_score = -1e30


def passed_along(value, axis, steps):
    count = lax.axis_size(axis)
    pairs = [(source, (source + steps) % count) for source in range(count)]
    return lax.ppermute(value, axis, pairs)


def attend(query_rows, key_rows, value_rows, allowed, score_scale):
    scores = (
        jnp.einsum("rkgd,nkd->kgrn", query_rows, key_rows, preferred_element_type=jnp.float32)
        * score_scale
    )
    scores = jnp.where(allowed[None, None], scores, masked_score)
    highest = jnp.max(scores, axis=-1)
    weights = jnp.where(allowed[None, None], jnp.exp(scores - highest[..., None]), 0.0)
    totals = jnp.sum(weights, axis=-1)
    summed = jnp.einsum(
        "kgrn,nkd->kgrd",
        weights.astype(jnp.bfloat16),
        value_rows,
        preferred_element_type=jnp.float32,
    )
    return (highest, totals, summed)


def combine_parts(earlier, later):
    larger = jnp.maximum(earlier[0], later[0])
    first_factor = jnp.exp(earlier[0] - larger)
    second_factor = jnp.exp(later[0] - larger)
    totals = earlier[1] * first_factor + later[1] * second_factor
    summed = earlier[2] * first_factor[..., None] + later[2] * second_factor[..., None]
    return (larger, totals, summed)


def on_device(
    queries, new_keys, new_values, cache_keys, cache_values, cache_lengths, turn_start, out_weight
):
    local_rows = queries.shape[0]
    kv_local = new_keys.shape[1] // HD
    group_size = H // KVH
    cache_dev = cache_keys.shape[1]
    score_scale = 1.0 / math.sqrt(HD)
    ctx_count = lax.axis_size("ctx")
    ctx_index = lax.axis_index("ctx")
    home_row = ctx_index * local_rows
    fresh_keys = new_keys.reshape(local_rows, kv_local, HD)
    fresh_values = new_values.reshape(local_rows, kv_local, HD)
    key_pos = (home_row + jnp.arange(local_rows, dtype=jnp.int32)) % NEW

    def partial_for(query_rows, first_row):
        traj_index = first_row // NEW
        stored_keys = lax.dynamic_index_in_dim(cache_keys, traj_index, 0, keepdims=False).reshape(
            cache_dev, kv_local, HD
        )
        stored_values = lax.dynamic_index_in_dim(
            cache_values, traj_index, 0, keepdims=False
        ).reshape(cache_dev, kv_local, HD)
        shard_fill = lax.dynamic_index_in_dim(cache_lengths, traj_index, 0, keepdims=False)[0]
        turn_begin = lax.dynamic_index_in_dim(turn_start, traj_index, 0, keepdims=False)
        row_count = query_rows.shape[0]
        query_pos = (first_row + jnp.arange(row_count, dtype=jnp.int32)) % NEW
        same_traj = home_row // NEW == traj_index
        new_ok = (
            same_traj & (key_pos[None, :] <= query_pos[:, None]) & (key_pos[None, :] >= turn_begin)
        )
        cache_ok = jnp.broadcast_to(
            (jnp.arange(cache_dev, dtype=jnp.int32) < shard_fill)[None, :], (row_count, cache_dev)
        )
        allowed = jnp.concatenate([cache_ok, new_ok], axis=1)
        key_rows = jnp.concatenate([stored_keys, fresh_keys], axis=0)
        value_rows = jnp.concatenate([stored_values, fresh_values], axis=0)
        return attend(query_rows, key_rows, value_rows, allowed, score_scale)

    query_block = queries.reshape(local_rows, kv_local, group_size, HD)
    start_state = (
        query_block,
        jnp.full((kv_local, group_size, local_rows), masked_score, jnp.float32),
        jnp.zeros((kv_local, group_size, local_rows), jnp.float32),
        jnp.zeros((kv_local, group_size, local_rows, HD), jnp.float32),
    )

    def cycle_step(step_index, cycle_state):
        moving, highest, totals, summed = cycle_state
        source = jnp.mod(ctx_index - step_index, ctx_count)
        fresh_part = partial_for(moving, source * local_rows)
        highest, totals, summed = combine_parts((highest, totals, summed), fresh_part)
        moving = passed_along(moving, "ctx", 1)
        highest, totals, summed = passed_along((highest, totals, summed), "ctx", 1)
        return (moving, highest, totals, summed)

    final_state = lax.fori_loop(0, ctx_count, cycle_step, start_state)
    highest, totals, summed = (final_state[1], final_state[2], final_state[3])
    attended = (
        (summed / totals[..., None])
        .transpose(2, 0, 1, 3)
        .reshape(local_rows, kv_local * group_size * HD)
        .astype(jnp.bfloat16)
    )
    return lax.psum_scatter(
        jnp.dot(attended, out_weight, preferred_element_type=jnp.float32).astype(jnp.bfloat16),
        "tp",
        scatter_dimension=0,
        tiled=True,
    )


def solution(mesh):
    in_specs = (
        P("ctx", "tp"),
        P("ctx", "tp"),
        P("ctx", "tp"),
        P(None, "ctx", "tp"),
        P(None, "ctx", "tp"),
        P(None, "ctx"),
        P(),
        P("tp", None),
    )
    out_specs = P(("ctx", "tp"), None)
    return jax.shard_map(
        on_device, mesh=mesh, in_specs=in_specs, out_specs=out_specs, check_vma=False
    )
```

profile of v0, /device:TPU:64, one launch (start us, length us, event | category | flops | bytes accessed | tf_op | source)
XLA Modules:
  0.0 702.6 jit_solution(8558075214841379355)
XLA Ops:
  7.6 645.0 %while.23 = (s32[]{:T(128)}, bf16[64,1,8,128]{3,0,2,1:T(8,128)(2,1)S(1)}, f32[1,8,64]{2,1,0:T(8,128)S(1)}, f32[1,8,64]{2,1,0:T(8,128)S(1)}, f32[1,8,64,128]{3,2,...) while((s32[]{:T(128)}, ...), condition=%wide.region_3.4_spmd.clone, body=%wide.region_0.3_spmd.clone.sunk | while | flops 224760928 | bytes 9151493 | solution.py:106
  13.3 1.3 fusion.41
  15.9 2.0 collective-permute-start.3
  17.9 3.1 collective-permute-start
  23.1 3.9 collective-permute-done.1
  32.7 1.3 fusion.41
  35.3 2.6 collective-permute-start.3
  37.9 3.7 collective-permute-start
  42.5 3.1 collective-permute-done.1
  51.4 1.3 fusion.41
  53.9 3.8 collective-permute-start.3
  57.7 3.7 collective-permute-start
  61.6 5.8 collective-permute-done.1
  76.5 3.7 collective-permute-start
  80.4 7.3 %collective-permute-done.1 = f32[1,8,64]{2,1,0:T(8,128)S(1)} collective-permute-done((f32[1,8,64]{2,1,0:T(8,128)S(1)}, f32[1,8,64]{2,1,0:T(8,128)S(1)}, u32[]{:S(2)}, u32[]{:S(2)}) %collective-permute-start.1) | collective-permute-done | bytes 2080 | tf_op jit(solution)/shard_map/while/body/eval_jaxpr/ppermute | solution.py:20
  93.4 1.3 fusion.41
  96.1 2.0 collective-permute-start
  99.0 8.1 %collective-permute-done.1 = f32[1,8,64]{2,1,0:T(8,128)S(1)} collective-permute-done((f32[1,8,64]{2,1,0:T(8,128)S(1)}, f32[1,8,64]{2,1,0:T(8,128)S(1)}, u32[]{:S(2)}, u32[]{:S(2)}) %collective-permute-start.1) | collective-permute-done | bytes 2080 | tf_op jit(solution)/shard_map/while/body/eval_jaxpr/ppermute | solution.py:20
  112.8 1.3 fusion.41
  115.7 2.3 collective-permute-start.1
  118.1 7.9 %collective-permute-done.1 = f32[1,8,64]{2,1,0:T(8,128)S(1)} collective-permute-done((f32[1,8,64]{2,1,0:T(8,128)S(1)}, f32[1,8,64]{2,1,0:T(8,128)S(1)}, u32[]{:S(2)}, u32[]{:S(2)}) %collective-permute-start.1) | collective-permute-done | bytes 2080 | tf_op jit(solution)/shard_map/while/body/eval_jaxpr/ppermute | solution.py:20
  131.8 1.3 fusion.41
  134.6 1.8 collective-permute-start.1
  136.5 9.0 %collective-permute-done.1 = f32[1,8,64]{2,1,0:T(8,128)S(1)} collective-permute-done((f32[1,8,64]{2,1,0:T(8,128)S(1)}, f32[1,8,64]{2,1,0:T(8,128)S(1)}, u32[]{:S(2)}, u32[]{:S(2)}) %collective-permute-start.1) | collective-permute-done | bytes 2080 | tf_op jit(solution)/shard_map/while/body/eval_jaxpr/ppermute | solution.py:20
  154.8 10.2 %collective-permute-done.1 = f32[1,8,64]{2,1,0:T(8,128)S(1)} collective-permute-done((f32[1,8,64]{2,1,0:T(8,128)S(1)}, f32[1,8,64]{2,1,0:T(8,128)S(1)}, u32[]{:S(2)}, u32[]{:S(2)}) %collective-permute-start.1) | collective-permute-done | bytes 2080 | tf_op jit(solution)/shard_map/while/body/eval_jaxpr/ppermute | solution.py:20
  170.8 1.3 fusion.41
  173.8 10.9 %collective-permute-done.1 = f32[1,8,64]{2,1,0:T(8,128)S(1)} collective-permute-done((f32[1,8,64]{2,1,0:T(8,128)S(1)}, f32[1,8,64]{2,1,0:T(8,128)S(1)}, u32[]{:S(2)}, u32[]{:S(2)}) %collective-permute-start.1) | collective-permute-done | bytes 2080 | tf_op jit(solution)/shard_map/while/body/eval_jaxpr/ppermute | solution.py:20
  190.4 1.3 fusion.41
  193.3 10.8 %collective-permute-done.1 = f32[1,8,64]{2,1,0:T(8,128)S(1)} collective-permute-done((f32[1,8,64]{2,1,0:T(8,128)S(1)}, f32[1,8,64]{2,1,0:T(8,128)S(1)}, u32[]{:S(2)}, u32[]{:S(2)}) %collective-permute-start.1) | collective-permute-done | bytes 2080 | tf_op jit(solution)/shard_map/while/body/eval_jaxpr/ppermute | solution.py:20
  210.0 1.3 fusion.41
  212.9 10.9 %collective-permute-done.1 = f32[1,8,64]{2,1,0:T(8,128)S(1)} collective-permute-done((f32[1,8,64]{2,1,0:T(8,128)S(1)}, f32[1,8,64]{2,1,0:T(8,128)S(1)}, u32[]{:S(2)}, u32[]{:S(2)}) %collective-permute-start.1) | collective-permute-done | bytes 2080 | tf_op jit(solution)/shard_map/while/body/eval_jaxpr/ppermute | solution.py:20
  232.5 10.9 %collective-permute-done.1 = f32[1,8,64]{2,1,0:T(8,128)S(1)} collective-permute-done((f32[1,8,64]{2,1,0:T(8,128)S(1)}, f32[1,8,64]{2,1,0:T(8,128)S(1)}, u32[]{:S(2)}, u32[]{:S(2)}) %collective-permute-start.1) | collective-permute-done | bytes 2080 | tf_op jit(solution)/shard_map/while/body/eval_jaxpr/ppermute | solution.py:20
  249.1 1.3 fusion.41
  252.0 10.9 %collective-permute-done.1 = f32[1,8,64]{2,1,0:T(8,128)S(1)} collective-permute-done((f32[1,8,64]{2,1,0:T(8,128)S(1)}, f32[1,8,64]{2,1,0:T(8,128)S(1)}, u32[]{:S(2)}, u32[]{:S(2)}) %collective-permute-start.1) | collective-permute-done | bytes 2080 | tf_op jit(solution)/shard_map/while/body/eval_jaxpr/ppermute | solution.py:20
  271.6 10.9 %collective-permute-done.1 = f32[1,8,64]{2,1,0:T(8,128)S(1)} collective-permute-done((f32[1,8,64]{2,1,0:T(8,128)S(1)}, f32[1,8,64]{2,1,0:T(8,128)S(1)}, u32[]{:S(2)}, u32[]{:S(2)}) %collective-permute-start.1) | collective-permute-done | bytes 2080 | tf_op jit(solution)/shard_map/while/body/eval_jaxpr/ppermute | solution.py:20
  288.3 1.3 fusion.41
  291.2 12.3 %collective-permute-done.1 = f32[1,8,64]{2,1,0:T(8,128)S(1)} collective-permute-done((f32[1,8,64]{2,1,0:T(8,128)S(1)}, f32[1,8,64]{2,1,0:T(8,128)S(1)}, u32[]{:S(2)}, u32[]{:S(2)}) %collective-permute-start.1) | collective-permute-done | bytes 2080 | tf_op jit(solution)/shard_map/while/body/eval_jaxpr/ppermute | solution.py:20
  309.4 1.3 fusion.41
  312.3 13.6 %collective-permute-done.1 = f32[1,8,64]{2,1,0:T(8,128)S(1)} collective-permute-done((f32[1,8,64]{2,1,0:T(8,128)S(1)}, f32[1,8,64]{2,1,0:T(8,128)S(1)}, u32[]{:S(2)}, u32[]{:S(2)}) %collective-permute-start.1) | collective-permute-done | bytes 2080 | tf_op jit(solution)/shard_map/while/body/eval_jaxpr/ppermute | solution.py:20
  334.6 14.8 %collective-permute-done.1 = f32[1,8,64]{2,1,0:T(8,128)S(1)} collective-permute-done((f32[1,8,64]{2,1,0:T(8,128)S(1)}, f32[1,8,64]{2,1,0:T(8,128)S(1)}, u32[]{:S(2)}, u32[]{:S(2)}) %collective-permute-start.1) | collective-permute-done | bytes 2080 | tf_op jit(solution)/shard_map/while/body/eval_jaxpr/ppermute | solution.py:20
  355.3 1.3 fusion.41
  358.2 15.5 %collective-permute-done.1 = f32[1,8,64]{2,1,0:T(8,128)S(1)} collective-permute-done((f32[1,8,64]{2,1,0:T(8,128)S(1)}, f32[1,8,64]{2,1,0:T(8,128)S(1)}, u32[]{:S(2)}, u32[]{:S(2)}) %collective-permute-start.1) | collective-permute-done | bytes 2080 | tf_op jit(solution)/shard_map/while/body/eval_jaxpr/ppermute | solution.py:20
  382.4 14.1 %collective-permute-done.1 = f32[1,8,64]{2,1,0:T(8,128)S(1)} collective-permute-done((f32[1,8,64]{2,1,0:T(8,128)S(1)}, f32[1,8,64]{2,1,0:T(8,128)S(1)}, u32[]{:S(2)}, u32[]{:S(2)}) %collective-permute-start.1) | collective-permute-done | bytes 2080 | tf_op jit(solution)/shard_map/while/body/eval_jaxpr/ppermute | solution.py:20
  405.2 12.6 %collective-permute-done.1 = f32[1,8,64]{2,1,0:T(8,128)S(1)} collective-permute-done((f32[1,8,64]{2,1,0:T(8,128)S(1)}, f32[1,8,64]{2,1,0:T(8,128)S(1)}, u32[]{:S(2)}, u32[]{:S(2)}) %collective-permute-start.1) | collective-permute-done | bytes 2080 | tf_op jit(solution)/shard_map/while/body/eval_jaxpr/ppermute | solution.py:20
  426.5 11.6 %collective-permute-done.1 = f32[1,8,64]{2,1,0:T(8,128)S(1)} collective-permute-done((f32[1,8,64]{2,1,0:T(8,128)S(1)}, f32[1,8,64]{2,1,0:T(8,128)S(1)}, u32[]{:S(2)}, u32[]{:S(2)}) %collective-permute-start.1) | collective-permute-done | bytes 2080 | tf_op jit(solution)/shard_map/while/body/eval_jaxpr/ppermute | solution.py:20
  446.8 10.8 %collective-permute-done.1 = f32[1,8,64]{2,1,0:T(8,128)S(1)} collective-permute-done((f32[1,8,64]{2,1,0:T(8,128)S(1)}, f32[1,8,64]{2,1,0:T(8,128)S(1)}, u32[]{:S(2)}, u32[]{:S(2)}) %collective-permute-start.1) | collective-permute-done | bytes 2080 | tf_op jit(solution)/shard_map/while/body/eval_jaxpr/ppermute | solution.py:20
  463.4 1.3 fusion.41
  466.3 10.3 %collective-permute-done.1 = f32[1,8,64]{2,1,0:T(8,128)S(1)} collective-permute-done((f32[1,8,64]{2,1,0:T(8,128)S(1)}, f32[1,8,64]{2,1,0:T(8,128)S(1)}, u32[]{:S(2)}, u32[]{:S(2)}) %collective-permute-start.1) | collective-permute-done | bytes 2080 | tf_op jit(solution)/shard_map/while/body/eval_jaxpr/ppermute | solution.py:20
  482.4 1.3 fusion.41
  485.3 10.7 %collective-permute-done.1 = f32[1,8,64]{2,1,0:T(8,128)S(1)} collective-permute-done((f32[1,8,64]{2,1,0:T(8,128)S(1)}, f32[1,8,64]{2,1,0:T(8,128)S(1)}, u32[]{:S(2)}, u32[]{:S(2)}) %collective-permute-start.1) | collective-permute-done | bytes 2080 | tf_op jit(solution)/shard_map/while/body/eval_jaxpr/ppermute | solution.py:20
  501.8 1.3 fusion.41
  504.7 10.9 %collective-permute-done.1 = f32[1,8,64]{2,1,0:T(8,128)S(1)} collective-permute-done((f32[1,8,64]{2,1,0:T(8,128)S(1)}, f32[1,8,64]{2,1,0:T(8,128)S(1)}, u32[]{:S(2)}, u32[]{:S(2)}) %collective-permute-start.1) | collective-permute-done | bytes 2080 | tf_op jit(solution)/shard_map/while/body/eval_jaxpr/ppermute | solution.py:20
  524.3 10.8 %collective-permute-done.1 = f32[1,8,64]{2,1,0:T(8,128)S(1)} collective-permute-done((f32[1,8,64]{2,1,0:T(8,128)S(1)}, f32[1,8,64]{2,1,0:T(8,128)S(1)}, u32[]{:S(2)}, u32[]{:S(2)}) %collective-permute-start.1) | collective-permute-done | bytes 2080 | tf_op jit(solution)/shard_map/while/body/eval_jaxpr/ppermute | solution.py:20
  540.9 1.3 fusion.41
  543.8 10.9 %collective-permute-done.1 = f32[1,8,64]{2,1,0:T(8,128)S(1)} collective-permute-done((f32[1,8,64]{2,1,0:T(8,128)S(1)}, f32[1,8,64]{2,1,0:T(8,128)S(1)}, u32[]{:S(2)}, u32[]{:S(2)}) %collective-permute-start.1) | collective-permute-done | bytes 2080 | tf_op jit(solution)/shard_map/while/body/eval_jaxpr/ppermute | solution.py:20
  563.4 10.9 %collective-permute-done.1 = f32[1,8,64]{2,1,0:T(8,128)S(1)} collective-permute-done((f32[1,8,64]{2,1,0:T(8,128)S(1)}, f32[1,8,64]{2,1,0:T(8,128)S(1)}, u32[]{:S(2)}, u32[]{:S(2)}) %collective-permute-start.1) | collective-permute-done | bytes 2080 | tf_op jit(solution)/shard_map/while/body/eval_jaxpr/ppermute | solution.py:20
  580.0 1.3 fusion.41
  583.0 10.9 %collective-permute-done.1 = f32[1,8,64]{2,1,0:T(8,128)S(1)} collective-permute-done((f32[1,8,64]{2,1,0:T(8,128)S(1)}, f32[1,8,64]{2,1,0:T(8,128)S(1)}, u32[]{:S(2)}, u32[]{:S(2)}) %collective-permute-start.1) | collective-permute-done | bytes 2080 | tf_op jit(solution)/shard_map/while/body/eval_jaxpr/ppermute | solution.py:20
  602.5 10.8 %collective-permute-done.1 = f32[1,8,64]{2,1,0:T(8,128)S(1)} collective-permute-done((f32[1,8,64]{2,1,0:T(8,128)S(1)}, f32[1,8,64]{2,1,0:T(8,128)S(1)}, u32[]{:S(2)}, u32[]{:S(2)}) %collective-permute-start.1) | collective-permute-done | bytes 2080 | tf_op jit(solution)/shard_map/while/body/eval_jaxpr/ppermute | solution.py:20
  619.2 1.3 fusion.41
  622.1 10.9 %collective-permute-done.1 = f32[1,8,64]{2,1,0:T(8,128)S(1)} collective-permute-done((f32[1,8,64]{2,1,0:T(8,128)S(1)}, f32[1,8,64]{2,1,0:T(8,128)S(1)}, u32[]{:S(2)}, u32[]{:S(2)}) %collective-permute-start.1) | collective-permute-done | bytes 2080 | tf_op jit(solution)/shard_map/while/body/eval_jaxpr/ppermute | solution.py:20
  641.7 10.9 %collective-permute-done.1 = f32[1,8,64]{2,1,0:T(8,128)S(1)} collective-permute-done((f32[1,8,64]{2,1,0:T(8,128)S(1)}, f32[1,8,64]{2,1,0:T(8,128)S(1)}, u32[]{:S(2)}, u32[]{:S(2)}) %collective-permute-start.1) | collective-permute-done | bytes 2080 | tf_op jit(solution)/shard_map/while/body/eval_jaxpr/ppermute | solution.py:20
  652.8 5.7 convolution_convert_fusion
  658.6 37.1 %reduce-scatter.2.cloned.1.call-done = bf16[8,4096]{1,0:T(8,128)(2,1)} async-done(((bf16[64,4096]{1,0:T(8,128)(2,1)}), bf16[8,4096]{1,0:T(8,128)(2,1)}) %reduce-scatter.2.cloned.1.call-update) | async-done | bytes 65552 | tf_op jit(solution)/shard_map/reduce_scatter | solution.py:114
  (780 shorter events, 254.8 us)
Async XLA Ops:
  6.5 689.2 %reduce-scatter.2.cloned.1.call-start = ((), (), s32[]{:S(2)}) async-start(), calls=%async_computation.1 | async-start | bytes 589824 | tf_op jit(solution)/shard_map/reduce_scatter | solution.py:114
  53.9 13.5 %collective-permute-start.3 = (f32[1,8,64,128]{3,2,1,0:T(8,128)S(1)}, f32[1,8,64,128]{3,2,1,0:T(8,128)S(1)}, u32[]{:S(2)}, u32[]{:S(2)}) collective-permute-start(f32[1,8,64,128]{3,2,1,0:T(8,128)S(1)} %fusion.44), channel_id=1, source_target_pairs={{0,8},{8,16},{16,24},{24,32},{32,40},{40,48},{48,56},{56,64},{64,7... | collective-permute-start | bytes 786440 | tf_op jit(solution)/shard_map/while/body/eval_jaxpr/ppermute | solution.py:20
  75.7 12.0 %collective-permute-start.3 = (f32[1,8,64,128]{3,2,1,0:T(8,128)S(1)}, f32[1,8,64,128]{3,2,1,0:T(8,128)S(1)}, u32[]{:S(2)}, u32[]{:S(2)}) collective-permute-start(f32[1,8,64,128]{3,2,1,0:T(8,128)S(1)} %fusion.44), channel_id=1, source_target_pairs={{0,8},{8,16},{16,24},{24,32},{32,40},{40,48},{48,56},{56,64},{64,7... | collective-permute-start | bytes 786440 | tf_op jit(solution)/shard_map/while/body/eval_jaxpr/ppermute | solution.py:20
  76.5 11.2 %collective-permute-start = (bf16[64,1,8,128]{3,0,2,1:T(8,128)(2,1)S(1)}, bf16[64,1,8,128]{3,0,2,1:T(8,128)(2,1)S(1)}, u32[]{:S(2)}, u32[]{:S(2)}) collective-permute-start(bf16[64,1,8,128]{3,0,2,1:T(8,128)(2,1)S(1)} %copy.23), channel_id=1, source_target_pairs={{0,8},{8,16},{16,24},{24,32},{32,40},{40,48},{48,56},{56,64},{64,7... | collective-permute-start | bytes 393224 | tf_op jit(solution)/shard_map/while/body/eval_jaxpr/ppermute | solution.py:20
  134.4 11.2 %collective-permute-start.3 = (f32[1,8,64,128]{3,2,1,0:T(8,128)S(1)}, f32[1,8,64,128]{3,2,1,0:T(8,128)S(1)}, u32[]{:S(2)}, u32[]{:S(2)}) collective-permute-start(f32[1,8,64,128]{3,2,1,0:T(8,128)S(1)} %fusion.44), channel_id=1, source_target_pairs={{0,8},{8,16},{16,24},{24,32},{32,40},{40,48},{48,56},{56,64},{64,7... | collective-permute-start | bytes 786440 | tf_op jit(solution)/shard_map/while/body/eval_jaxpr/ppermute | solution.py:20
  153.8 11.3 %collective-permute-start.3 = (f32[1,8,64,128]{3,2,1,0:T(8,128)S(1)}, f32[1,8,64,128]{3,2,1,0:T(8,128)S(1)}, u32[]{:S(2)}, u32[]{:S(2)}) collective-permute-start(f32[1,8,64,128]{3,2,1,0:T(8,128)S(1)} %fusion.44), channel_id=1, source_target_pairs={{0,8},{8,16},{16,24},{24,32},{32,40},{40,48},{48,56},{56,64},{64,7... | collective-permute-start | bytes 786440 | tf_op jit(solution)/shard_map/while/body/eval_jaxpr/ppermute | solution.py:20
  153.9 11.2 %collective-permute-start = (bf16[64,1,8,128]{3,0,2,1:T(8,128)(2,1)S(1)}, bf16[64,1,8,128]{3,0,2,1:T(8,128)(2,1)S(1)}, u32[]{:S(2)}, u32[]{:S(2)}) collective-permute-start(bf16[64,1,8,128]{3,0,2,1:T(8,128)(2,1)S(1)} %copy.23), channel_id=1, source_target_pairs={{0,8},{8,16},{16,24},{24,32},{32,40},{40,48},{48,56},{56,64},{64,7... | collective-permute-start | bytes 393224 | tf_op jit(solution)/shard_map/while/body/eval_jaxpr/ppermute | solution.py:20
  173.4 11.3 %collective-permute-start.3 = (f32[1,8,64,128]{3,2,1,0:T(8,128)S(1)}, f32[1,8,64,128]{3,2,1,0:T(8,128)S(1)}, u32[]{:S(2)}, u32[]{:S(2)}) collective-permute-start(f32[1,8,64,128]{3,2,1,0:T(8,128)S(1)} %fusion.44), channel_id=1, source_target_pairs={{0,8},{8,16},{16,24},{24,32},{32,40},{40,48},{48,56},{56,64},{64,7... | collective-permute-start | bytes 786440 | tf_op jit(solution)/shard_map/while/body/eval_jaxpr/ppermute | solution.py:20
  173.5 11.2 %collective-permute-start = (bf16[64,1,8,128]{3,0,2,1:T(8,128)(2,1)S(1)}, bf16[64,1,8,128]{3,0,2,1:T(8,128)(2,1)S(1)}, u32[]{:S(2)}, u32[]{:S(2)}) collective-permute-start(bf16[64,1,8,128]{3,0,2,1:T(8,128)(2,1)S(1)} %copy.23), channel_id=1, source_target_pairs={{0,8},{8,16},{16,24},{24,32},{32,40},{40,48},{48,56},{56,64},{64,7... | collective-permute-start | bytes 393224 | tf_op jit(solution)/shard_map/while/body/eval_jaxpr/ppermute | solution.py:20
  193.0 11.3 %collective-permute-start.3 = (f32[1,8,64,128]{3,2,1,0:T(8,128)S(1)}, f32[1,8,64,128]{3,2,1,0:T(8,128)S(1)}, u32[]{:S(2)}, u32[]{:S(2)}) collective-permute-start(f32[1,8,64,128]{3,2,1,0:T(8,128)S(1)} %fusion.44), channel_id=1, source_target_pairs={{0,8},{8,16},{16,24},{24,32},{32,40},{40,48},{48,56},{56,64},{64,7... | collective-permute-start | bytes 786440 | tf_op jit(solution)/shard_map/while/body/eval_jaxpr/ppermute | solution.py:20
  193.1 11.2 %collective-permute-start = (bf16[64,1,8,128]{3,0,2,1:T(8,128)(2,1)S(1)}, bf16[64,1,8,128]{3,0,2,1:T(8,128)(2,1)S(1)}, u32[]{:S(2)}, u32[]{:S(2)}) collective-permute-start(bf16[64,1,8,128]{3,0,2,1:T(8,128)(2,1)S(1)} %copy.23), channel_id=1, source_target_pairs={{0,8},{8,16},{16,24},{24,32},{32,40},{40,48},{48,56},{56,64},{64,7... | collective-permute-start | bytes 393224 | tf_op jit(solution)/shard_map/while/body/eval_jaxpr/ppermute | solution.py:20
  212.5 11.3 %collective-permute-start.3 = (f32[1,8,64,128]{3,2,1,0:T(8,128)S(1)}, f32[1,8,64,128]{3,2,1,0:T(8,128)S(1)}, u32[]{:S(2)}, u32[]{:S(2)}) collective-permute-start(f32[1,8,64,128]{3,2,1,0:T(8,128)S(1)} %fusion.44), channel_id=1, source_target_pairs={{0,8},{8,16},{16,24},{24,32},{32,40},{40,48},{48,56},{56,64},{64,7... | collective-permute-start | bytes 786440 | tf_op jit(solution)/shard_map/while/body/eval_jaxpr/ppermute | solution.py:20
  212.6 11.2 %collective-permute-start = (bf16[64,1,8,128]{3,0,2,1:T(8,128)(2,1)S(1)}, bf16[64,1,8,128]{3,0,2,1:T(8,128)(2,1)S(1)}, u32[]{:S(2)}, u32[]{:S(2)}) collective-permute-start(bf16[64,1,8,128]{3,0,2,1:T(8,128)(2,1)S(1)} %copy.23), channel_id=1, source_target_pairs={{0,8},{8,16},{16,24},{24,32},{32,40},{40,48},{48,56},{56,64},{64,7... | collective-permute-start | bytes 393224 | tf_op jit(solution)/shard_map/while/body/eval_jaxpr/ppermute | solution.py:20
  232.1 11.3 %collective-permute-start.3 = (f32[1,8,64,128]{3,2,1,0:T(8,128)S(1)}, f32[1,8,64,128]{3,2,1,0:T(8,128)S(1)}, u32[]{:S(2)}, u32[]{:S(2)}) collective-permute-start(f32[1,8,64,128]{3,2,1,0:T(8,128)S(1)} %fusion.44), channel_id=1, source_target_pairs={{0,8},{8,16},{16,24},{24,32},{32,40},{40,48},{48,56},{56,64},{64,7... | collective-permute-start | bytes 786440 | tf_op jit(solution)/shard_map/while/body/eval_jaxpr/ppermute | solution.py:20
  232.2 11.2 %collective-permute-start = (bf16[64,1,8,128]{3,0,2,1:T(8,128)(2,1)S(1)}, bf16[64,1,8,128]{3,0,2,1:T(8,128)(2,1)S(1)}, u32[]{:S(2)}, u32[]{:S(2)}) collective-permute-start(bf16[64,1,8,128]{3,0,2,1:T(8,128)(2,1)S(1)} %copy.23), channel_id=1, source_target_pairs={{0,8},{8,16},{16,24},{24,32},{32,40},{40,48},{48,56},{56,64},{64,7... | collective-permute-start | bytes 393224 | tf_op jit(solution)/shard_map/while/body/eval_jaxpr/ppermute | solution.py:20
  251.7 11.3 %collective-permute-start.3 = (f32[1,8,64,128]{3,2,1,0:T(8,128)S(1)}, f32[1,8,64,128]{3,2,1,0:T(8,128)S(1)}, u32[]{:S(2)}, u32[]{:S(2)}) collective-permute-start(f32[1,8,64,128]{3,2,1,0:T(8,128)S(1)} %fusion.44), channel_id=1, source_target_pairs={{0,8},{8,16},{16,24},{24,32},{32,40},{40,48},{48,56},{56,64},{64,7... | collective-permute-start | bytes 786440 | tf_op jit(solution)/shard_map/while/body/eval_jaxpr/ppermute | solution.py:20
  251.8 11.2 %collective-permute-start = (bf16[64,1,8,128]{3,0,2,1:T(8,128)(2,1)S(1)}, bf16[64,1,8,128]{3,0,2,1:T(8,128)(2,1)S(1)}, u32[]{:S(2)}, u32[]{:S(2)}) collective-permute-start(bf16[64,1,8,128]{3,0,2,1:T(8,128)(2,1)S(1)} %copy.23), channel_id=1, source_target_pairs={{0,8},{8,16},{16,24},{24,32},{32,40},{40,48},{48,56},{56,64},{64,7... | collective-permute-start | bytes 393224 | tf_op jit(solution)/shard_map/while/body/eval_jaxpr/ppermute | solution.py:20
  271.2 11.3 %collective-permute-start.3 = (f32[1,8,64,128]{3,2,1,0:T(8,128)S(1)}, f32[1,8,64,128]{3,2,1,0:T(8,128)S(1)}, u32[]{:S(2)}, u32[]{:S(2)}) collective-permute-start(f32[1,8,64,128]{3,2,1,0:T(8,128)S(1)} %fusion.44), channel_id=1, source_target_pairs={{0,8},{8,16},{16,24},{24,32},{32,40},{40,48},{48,56},{56,64},{64,7... | collective-permute-start | bytes 786440 | tf_op jit(solution)/shard_map/while/body/eval_jaxpr/ppermute | solution.py:20
  271.3 11.2 %collective-permute-start = (bf16[64,1,8,128]{3,0,2,1:T(8,128)(2,1)S(1)}, bf16[64,1,8,128]{3,0,2,1:T(8,128)(2,1)S(1)}, u32[]{:S(2)}, u32[]{:S(2)}) collective-permute-start(bf16[64,1,8,128]{3,0,2,1:T(8,128)(2,1)S(1)} %copy.23), channel_id=1, source_target_pairs={{0,8},{8,16},{16,24},{24,32},{32,40},{40,48},{48,56},{56,64},{64,7... | collective-permute-start | bytes 393224 | tf_op jit(solution)/shard_map/while/body/eval_jaxpr/ppermute | solution.py:20
  290.9 12.8 %collective-permute-start.3 = (f32[1,8,64,128]{3,2,1,0:T(8,128)S(1)}, f32[1,8,64,128]{3,2,1,0:T(8,128)S(1)}, u32[]{:S(2)}, u32[]{:S(2)}) collective-permute-start(f32[1,8,64,128]{3,2,1,0:T(8,128)S(1)} %fusion.44), channel_id=1, source_target_pairs={{0,8},{8,16},{16,24},{24,32},{32,40},{40,48},{48,56},{56,64},{64,7... | collective-permute-start | bytes 786440 | tf_op jit(solution)/shard_map/while/body/eval_jaxpr/ppermute | solution.py:20
  291.0 12.7 %collective-permute-start = (bf16[64,1,8,128]{3,0,2,1:T(8,128)(2,1)S(1)}, bf16[64,1,8,128]{3,0,2,1:T(8,128)(2,1)S(1)}, u32[]{:S(2)}, u32[]{:S(2)}) collective-permute-start(bf16[64,1,8,128]{3,0,2,1:T(8,128)(2,1)S(1)} %copy.23), channel_id=1, source_target_pairs={{0,8},{8,16},{16,24},{24,32},{32,40},{40,48},{48,56},{56,64},{64,7... | collective-permute-start | bytes 393224 | tf_op jit(solution)/shard_map/while/body/eval_jaxpr/ppermute | solution.py:20
  291.1 12.5 %collective-permute-start.1 = (f32[1,8,64]{2,1,0:T(8,128)S(1)}, f32[1,8,64]{2,1,0:T(8,128)S(1)}, u32[]{:S(2)}, u32[]{:S(2)}) collective-permute-start(f32[1,8,64]{2,1,0:T(8,128)S(1)} %get-tuple-element.614), channel_id=1, source_target_pairs={{0,8},{8,16},{16,24},{24,32},{32,40},{40,48},{48,56},{56,64},{64,7... | collective-permute-start | bytes 6152 | tf_op jit(solution)/shard_map/while/body/eval_jaxpr/ppermute | solution.py:20
  291.1 12.5 %collective-permute-start.2 = (f32[1,8,64]{2,1,0:T(8,128)S(1)}, f32[1,8,64]{2,1,0:T(8,128)S(1)}, u32[]{:S(2)}, u32[]{:S(2)}) collective-permute-start(f32[1,8,64]{2,1,0:T(8,128)S(1)} %get-tuple-element.615), channel_id=1, source_target_pairs={{0,8},{8,16},{16,24},{24,32},{32,40},{40,48},{48,56},{56,64},{64,7... | collective-permute-start | bytes 6152 | tf_op jit(solution)/shard_map/while/body/eval_jaxpr/ppermute | solution.py:20
  311.9 14.1 %collective-permute-start.3 = (f32[1,8,64,128]{3,2,1,0:T(8,128)S(1)}, f32[1,8,64,128]{3,2,1,0:T(8,128)S(1)}, u32[]{:S(2)}, u32[]{:S(2)}) collective-permute-start(f32[1,8,64,128]{3,2,1,0:T(8,128)S(1)} %fusion.44), channel_id=1, source_target_pairs={{0,8},{8,16},{16,24},{24,32},{32,40},{40,48},{48,56},{56,64},{64,7... | collective-permute-start | bytes 786440 | tf_op jit(solution)/shard_map/while/body/eval_jaxpr/ppermute | solution.py:20
  312.0 14.0 %collective-permute-start = (bf16[64,1,8,128]{3,0,2,1:T(8,128)(2,1)S(1)}, bf16[64,1,8,128]{3,0,2,1:T(8,128)(2,1)S(1)}, u32[]{:S(2)}, u32[]{:S(2)}) collective-permute-start(bf16[64,1,8,128]{3,0,2,1:T(8,128)(2,1)S(1)} %copy.23), channel_id=1, source_target_pairs={{0,8},{8,16},{16,24},{24,32},{32,40},{40,48},{48,56},{56,64},{64,7... | collective-permute-start | bytes 393224 | tf_op jit(solution)/shard_map/while/body/eval_jaxpr/ppermute | solution.py:20
  312.1 13.8 %collective-permute-start.1 = (f32[1,8,64]{2,1,0:T(8,128)S(1)}, f32[1,8,64]{2,1,0:T(8,128)S(1)}, u32[]{:S(2)}, u32[]{:S(2)}) collective-permute-start(f32[1,8,64]{2,1,0:T(8,128)S(1)} %get-tuple-element.614), channel_id=1, source_target_pairs={{0,8},{8,16},{16,24},{24,32},{32,40},{40,48},{48,56},{56,64},{64,7... | collective-permute-start | bytes 6152 | tf_op jit(solution)/shard_map/while/body/eval_jaxpr/ppermute | solution.py:20
  312.2 13.8 %collective-permute-start.2 = (f32[1,8,64]{2,1,0:T(8,128)S(1)}, f32[1,8,64]{2,1,0:T(8,128)S(1)}, u32[]{:S(2)}, u32[]{:S(2)}) collective-permute-start(f32[1,8,64]{2,1,0:T(8,128)S(1)} %get-tuple-element.615), channel_id=1, source_target_pairs={{0,8},{8,16},{16,24},{24,32},{32,40},{40,48},{48,56},{56,64},{64,7... | collective-permute-start | bytes 6152 | tf_op jit(solution)/shard_map/while/body/eval_jaxpr/ppermute | solution.py:20
  334.3 15.2 %collective-permute-start.3 = (f32[1,8,64,128]{3,2,1,0:T(8,128)S(1)}, f32[1,8,64,128]{3,2,1,0:T(8,128)S(1)}, u32[]{:S(2)}, u32[]{:S(2)}) collective-permute-start(f32[1,8,64,128]{3,2,1,0:T(8,128)S(1)} %fusion.44), channel_id=1, source_target_pairs={{0,8},{8,16},{16,24},{24,32},{32,40},{40,48},{48,56},{56,64},{64,7... | collective-permute-start | bytes 786440 | tf_op jit(solution)/shard_map/while/body/eval_jaxpr/ppermute | solution.py:20
  334.4 15.2 %collective-permute-start = (bf16[64,1,8,128]{3,0,2,1:T(8,128)(2,1)S(1)}, bf16[64,1,8,128]{3,0,2,1:T(8,128)(2,1)S(1)}, u32[]{:S(2)}, u32[]{:S(2)}) collective-permute-start(bf16[64,1,8,128]{3,0,2,1:T(8,128)(2,1)S(1)} %copy.23), channel_id=1, source_target_pairs={{0,8},{8,16},{16,24},{24,32},{32,40},{40,48},{48,56},{56,64},{64,7... | collective-permute-start | bytes 393224 | tf_op jit(solution)/shard_map/while/body/eval_jaxpr/ppermute | solution.py:20
  334.5 15.0 %collective-permute-start.1 = (f32[1,8,64]{2,1,0:T(8,128)S(1)}, f32[1,8,64]{2,1,0:T(8,128)S(1)}, u32[]{:S(2)}, u32[]{:S(2)}) collective-permute-start(f32[1,8,64]{2,1,0:T(8,128)S(1)} %get-tuple-element.614), channel_id=1, source_target_pairs={{0,8},{8,16},{16,24},{24,32},{32,40},{40,48},{48,56},{56,64},{64,7... | collective-permute-start | bytes 6152 | tf_op jit(solution)/shard_map/while/body/eval_jaxpr/ppermute | solution.py:20
  334.6 15.0 %collective-permute-start.2 = (f32[1,8,64]{2,1,0:T(8,128)S(1)}, f32[1,8,64]{2,1,0:T(8,128)S(1)}, u32[]{:S(2)}, u32[]{:S(2)}) collective-permute-start(f32[1,8,64]{2,1,0:T(8,128)S(1)} %get-tuple-element.615), channel_id=1, source_target_pairs={{0,8},{8,16},{16,24},{24,32},{32,40},{40,48},{48,56},{56,64},{64,7... | collective-permute-start | bytes 6152 | tf_op jit(solution)/shard_map/while/body/eval_jaxpr/ppermute | solution.py:20
  357.8 15.9 %collective-permute-start.3 = (f32[1,8,64,128]{3,2,1,0:T(8,128)S(1)}, f32[1,8,64,128]{3,2,1,0:T(8,128)S(1)}, u32[]{:S(2)}, u32[]{:S(2)}) collective-permute-start(f32[1,8,64,128]{3,2,1,0:T(8,128)S(1)} %fusion.44), channel_id=1, source_target_pairs={{0,8},{8,16},{16,24},{24,32},{32,40},{40,48},{48,56},{56,64},{64,7... | collective-permute-start | bytes 786440 | tf_op jit(solution)/shard_map/while/body/eval_jaxpr/ppermute | solution.py:20
  357.9 15.8 %collective-permute-start = (bf16[64,1,8,128]{3,0,2,1:T(8,128)(2,1)S(1)}, bf16[64,1,8,128]{3,0,2,1:T(8,128)(2,1)S(1)}, u32[]{:S(2)}, u32[]{:S(2)}) collective-permute-start(bf16[64,1,8,128]{3,0,2,1:T(8,128)(2,1)S(1)} %copy.23), channel_id=1, source_target_pairs={{0,8},{8,16},{16,24},{24,32},{32,40},{40,48},{48,56},{56,64},{64,7... | collective-permute-start | bytes 393224 | tf_op jit(solution)/shard_map/while/body/eval_jaxpr/ppermute | solution.py:20
  358.0 15.6 %collective-permute-start.1 = (f32[1,8,64]{2,1,0:T(8,128)S(1)}, f32[1,8,64]{2,1,0:T(8,128)S(1)}, u32[]{:S(2)}, u32[]{:S(2)}) collective-permute-start(f32[1,8,64]{2,1,0:T(8,128)S(1)} %get-tuple-element.614), channel_id=1, source_target_pairs={{0,8},{8,16},{16,24},{24,32},{32,40},{40,48},{48,56},{56,64},{64,7... | collective-permute-start | bytes 6152 | tf_op jit(solution)/shard_map/while/body/eval_jaxpr/ppermute | solution.py:20
  358.1 15.6 %collective-permute-start.2 = (f32[1,8,64]{2,1,0:T(8,128)S(1)}, f32[1,8,64]{2,1,0:T(8,128)S(1)}, u32[]{:S(2)}, u32[]{:S(2)}) collective-permute-start(f32[1,8,64]{2,1,0:T(8,128)S(1)} %get-tuple-element.615), channel_id=1, source_target_pairs={{0,8},{8,16},{16,24},{24,32},{32,40},{40,48},{48,56},{56,64},{64,7... | collective-permute-start | bytes 6152 | tf_op jit(solution)/shard_map/while/body/eval_jaxpr/ppermute | solution.py:20
  382.0 14.5 %collective-permute-start.3 = (f32[1,8,64,128]{3,2,1,0:T(8,128)S(1)}, f32[1,8,64,128]{3,2,1,0:T(8,128)S(1)}, u32[]{:S(2)}, u32[]{:S(2)}) collective-permute-start(f32[1,8,64,128]{3,2,1,0:T(8,128)S(1)} %fusion.44), channel_id=1, source_target_pairs={{0,8},{8,16},{16,24},{24,32},{32,40},{40,48},{48,56},{56,64},{64,7... | collective-permute-start | bytes 786440 | tf_op jit(solution)/shard_map/while/body/eval_jaxpr/ppermute | solution.py:20
  382.1 14.5 %collective-permute-start = (bf16[64,1,8,128]{3,0,2,1:T(8,128)(2,1)S(1)}, bf16[64,1,8,128]{3,0,2,1:T(8,128)(2,1)S(1)}, u32[]{:S(2)}, u32[]{:S(2)}) collective-permute-start(bf16[64,1,8,128]{3,0,2,1:T(8,128)(2,1)S(1)} %copy.23), channel_id=1, source_target_pairs={{0,8},{8,16},{16,24},{24,32},{32,40},{40,48},{48,56},{56,64},{64,7... | collective-permute-start | bytes 393224 | tf_op jit(solution)/shard_map/while/body/eval_jaxpr/ppermute | solution.py:20
  382.2 14.3 %collective-permute-start.1 = (f32[1,8,64]{2,1,0:T(8,128)S(1)}, f32[1,8,64]{2,1,0:T(8,128)S(1)}, u32[]{:S(2)}, u32[]{:S(2)}) collective-permute-start(f32[1,8,64]{2,1,0:T(8,128)S(1)} %get-tuple-element.614), channel_id=1, source_target_pairs={{0,8},{8,16},{16,24},{24,32},{32,40},{40,48},{48,56},{56,64},{64,7... | collective-permute-start | bytes 6152 | tf_op jit(solution)/shard_map/while/body/eval_jaxpr/ppermute | solution.py:20
  382.3 14.3 %collective-permute-start.2 = (f32[1,8,64]{2,1,0:T(8,128)S(1)}, f32[1,8,64]{2,1,0:T(8,128)S(1)}, u32[]{:S(2)}, u32[]{:S(2)}) collective-permute-start(f32[1,8,64]{2,1,0:T(8,128)S(1)} %get-tuple-element.615), channel_id=1, source_target_pairs={{0,8},{8,16},{16,24},{24,32},{32,40},{40,48},{48,56},{56,64},{64,7... | collective-permute-start | bytes 6152 | tf_op jit(solution)/shard_map/while/body/eval_jaxpr/ppermute | solution.py:20
  404.8 13.0 %collective-permute-start.3 = (f32[1,8,64,128]{3,2,1,0:T(8,128)S(1)}, f32[1,8,64,128]{3,2,1,0:T(8,128)S(1)}, u32[]{:S(2)}, u32[]{:S(2)}) collective-permute-start(f32[1,8,64,128]{3,2,1,0:T(8,128)S(1)} %fusion.44), channel_id=1, source_target_pairs={{0,8},{8,16},{16,24},{24,32},{32,40},{40,48},{48,56},{56,64},{64,7... | collective-permute-start | bytes 786440 | tf_op jit(solution)/shard_map/while/body/eval_jaxpr/ppermute | solution.py:20
  404.9 12.9 %collective-permute-start = (bf16[64,1,8,128]{3,0,2,1:T(8,128)(2,1)S(1)}, bf16[64,1,8,128]{3,0,2,1:T(8,128)(2,1)S(1)}, u32[]{:S(2)}, u32[]{:S(2)}) collective-permute-start(bf16[64,1,8,128]{3,0,2,1:T(8,128)(2,1)S(1)} %copy.23), channel_id=1, source_target_pairs={{0,8},{8,16},{16,24},{24,32},{32,40},{40,48},{48,56},{56,64},{64,7... | collective-permute-start | bytes 393224 | tf_op jit(solution)/shard_map/while/body/eval_jaxpr/ppermute | solution.py:20
  405.0 12.8 %collective-permute-start.1 = (f32[1,8,64]{2,1,0:T(8,128)S(1)}, f32[1,8,64]{2,1,0:T(8,128)S(1)}, u32[]{:S(2)}, u32[]{:S(2)}) collective-permute-start(f32[1,8,64]{2,1,0:T(8,128)S(1)} %get-tuple-element.614), channel_id=1, source_target_pairs={{0,8},{8,16},{16,24},{24,32},{32,40},{40,48},{48,56},{56,64},{64,7... | collective-permute-start | bytes 6152 | tf_op jit(solution)/shard_map/while/body/eval_jaxpr/ppermute | solution.py:20
  405.1 12.7 %collective-permute-start.2 = (f32[1,8,64]{2,1,0:T(8,128)S(1)}, f32[1,8,64]{2,1,0:T(8,128)S(1)}, u32[]{:S(2)}, u32[]{:S(2)}) collective-permute-start(f32[1,8,64]{2,1,0:T(8,128)S(1)} %get-tuple-element.615), channel_id=1, source_target_pairs={{0,8},{8,16},{16,24},{24,32},{32,40},{40,48},{48,56},{56,64},{64,7... | collective-permute-start | bytes 6152 | tf_op jit(solution)/shard_map/while/body/eval_jaxpr/ppermute | solution.py:20
  426.1 12.1 %collective-permute-start.3 = (f32[1,8,64,128]{3,2,1,0:T(8,128)S(1)}, f32[1,8,64,128]{3,2,1,0:T(8,128)S(1)}, u32[]{:S(2)}, u32[]{:S(2)}) collective-permute-start(f32[1,8,64,128]{3,2,1,0:T(8,128)S(1)} %fusion.44), channel_id=1, source_target_pairs={{0,8},{8,16},{16,24},{24,32},{32,40},{40,48},{48,56},{56,64},{64,7... | collective-permute-start | bytes 786440 | tf_op jit(solution)/shard_map/while/body/eval_jaxpr/ppermute | solution.py:20
  426.2 12.0 %collective-permute-start = (bf16[64,1,8,128]{3,0,2,1:T(8,128)(2,1)S(1)}, bf16[64,1,8,128]{3,0,2,1:T(8,128)(2,1)S(1)}, u32[]{:S(2)}, u32[]{:S(2)}) collective-permute-start(bf16[64,1,8,128]{3,0,2,1:T(8,128)(2,1)S(1)} %copy.23), channel_id=1, source_target_pairs={{0,8},{8,16},{16,24},{24,32},{32,40},{40,48},{48,56},{56,64},{64,7... | collective-permute-start | bytes 393224 | tf_op jit(solution)/shard_map/while/body/eval_jaxpr/ppermute | solution.py:20
  426.3 11.8 %collective-permute-start.1 = (f32[1,8,64]{2,1,0:T(8,128)S(1)}, f32[1,8,64]{2,1,0:T(8,128)S(1)}, u32[]{:S(2)}, u32[]{:S(2)}) collective-permute-start(f32[1,8,64]{2,1,0:T(8,128)S(1)} %get-tuple-element.614), channel_id=1, source_target_pairs={{0,8},{8,16},{16,24},{24,32},{32,40},{40,48},{48,56},{56,64},{64,7... | collective-permute-start | bytes 6152 | tf_op jit(solution)/shard_map/while/body/eval_jaxpr/ppermute | solution.py:20
  426.4 11.8 %collective-permute-start.2 = (f32[1,8,64]{2,1,0:T(8,128)S(1)}, f32[1,8,64]{2,1,0:T(8,128)S(1)}, u32[]{:S(2)}, u32[]{:S(2)}) collective-permute-start(f32[1,8,64]{2,1,0:T(8,128)S(1)} %get-tuple-element.615), channel_id=1, source_target_pairs={{0,8},{8,16},{16,24},{24,32},{32,40},{40,48},{48,56},{56,64},{64,7... | collective-permute-start | bytes 6152 | tf_op jit(solution)/shard_map/while/body/eval_jaxpr/ppermute | solution.py:20
  446.5 11.2 %collective-permute-start.3 = (f32[1,8,64,128]{3,2,1,0:T(8,128)S(1)}, f32[1,8,64,128]{3,2,1,0:T(8,128)S(1)}, u32[]{:S(2)}, u32[]{:S(2)}) collective-permute-start(f32[1,8,64,128]{3,2,1,0:T(8,128)S(1)} %fusion.44), channel_id=1, source_target_pairs={{0,8},{8,16},{16,24},{24,32},{32,40},{40,48},{48,56},{56,64},{64,7... | collective-permute-start | bytes 786440 | tf_op jit(solution)/shard_map/while/body/eval_jaxpr/ppermute | solution.py:20
  504.3 11.3 %collective-permute-start.3 = (f32[1,8,64,128]{3,2,1,0:T(8,128)S(1)}, f32[1,8,64,128]{3,2,1,0:T(8,128)S(1)}, u32[]{:S(2)}, u32[]{:S(2)}) collective-permute-start(f32[1,8,64,128]{3,2,1,0:T(8,128)S(1)} %fusion.44), channel_id=1, source_target_pairs={{0,8},{8,16},{16,24},{24,32},{32,40},{40,48},{48,56},{56,64},{64,7... | collective-permute-start | bytes 786440 | tf_op jit(solution)/shard_map/while/body/eval_jaxpr/ppermute | solution.py:20
  504.4 11.2 %collective-permute-start = (bf16[64,1,8,128]{3,0,2,1:T(8,128)(2,1)S(1)}, bf16[64,1,8,128]{3,0,2,1:T(8,128)(2,1)S(1)}, u32[]{:S(2)}, u32[]{:S(2)}) collective-permute-start(bf16[64,1,8,128]{3,0,2,1:T(8,128)(2,1)S(1)} %copy.23), channel_id=1, source_target_pairs={{0,8},{8,16},{16,24},{24,32},{32,40},{40,48},{48,56},{56,64},{64,7... | collective-permute-start | bytes 393224 | tf_op jit(solution)/shard_map/while/body/eval_jaxpr/ppermute | solution.py:20
  523.9 11.3 %collective-permute-start.3 = (f32[1,8,64,128]{3,2,1,0:T(8,128)S(1)}, f32[1,8,64,128]{3,2,1,0:T(8,128)S(1)}, u32[]{:S(2)}, u32[]{:S(2)}) collective-permute-start(f32[1,8,64,128]{3,2,1,0:T(8,128)S(1)} %fusion.44), channel_id=1, source_target_pairs={{0,8},{8,16},{16,24},{24,32},{32,40},{40,48},{48,56},{56,64},{64,7... | collective-permute-start | bytes 786440 | tf_op jit(solution)/shard_map/while/body/eval_jaxpr/ppermute | solution.py:20
  524.0 11.2 %collective-permute-start = (bf16[64,1,8,128]{3,0,2,1:T(8,128)(2,1)S(1)}, bf16[64,1,8,128]{3,0,2,1:T(8,128)(2,1)S(1)}, u32[]{:S(2)}, u32[]{:S(2)}) collective-permute-start(bf16[64,1,8,128]{3,0,2,1:T(8,128)(2,1)S(1)} %copy.23), channel_id=1, source_target_pairs={{0,8},{8,16},{16,24},{24,32},{32,40},{40,48},{48,56},{56,64},{64,7... | collective-permute-start | bytes 393224 | tf_op jit(solution)/shard_map/while/body/eval_jaxpr/ppermute | solution.py:20
  543.5 11.3 %collective-permute-start.3 = (f32[1,8,64,128]{3,2,1,0:T(8,128)S(1)}, f32[1,8,64,128]{3,2,1,0:T(8,128)S(1)}, u32[]{:S(2)}, u32[]{:S(2)}) collective-permute-start(f32[1,8,64,128]{3,2,1,0:T(8,128)S(1)} %fusion.44), channel_id=1, source_target_pairs={{0,8},{8,16},{16,24},{24,32},{32,40},{40,48},{48,56},{56,64},{64,7... | collective-permute-start | bytes 786440 | tf_op jit(solution)/shard_map/while/body/eval_jaxpr/ppermute | solution.py:20
  543.6 11.2 %collective-permute-start = (bf16[64,1,8,128]{3,0,2,1:T(8,128)(2,1)S(1)}, bf16[64,1,8,128]{3,0,2,1:T(8,128)(2,1)S(1)}, u32[]{:S(2)}, u32[]{:S(2)}) collective-permute-start(bf16[64,1,8,128]{3,0,2,1:T(8,128)(2,1)S(1)} %copy.23), channel_id=1, source_target_pairs={{0,8},{8,16},{16,24},{24,32},{32,40},{40,48},{48,56},{56,64},{64,7... | collective-permute-start | bytes 393224 | tf_op jit(solution)/shard_map/while/body/eval_jaxpr/ppermute | solution.py:20
  563.0 11.3 %collective-permute-start.3 = (f32[1,8,64,128]{3,2,1,0:T(8,128)S(1)}, f32[1,8,64,128]{3,2,1,0:T(8,128)S(1)}, u32[]{:S(2)}, u32[]{:S(2)}) collective-permute-start(f32[1,8,64,128]{3,2,1,0:T(8,128)S(1)} %fusion.44), channel_id=1, source_target_pairs={{0,8},{8,16},{16,24},{24,32},{32,40},{40,48},{48,56},{56,64},{64,7... | collective-permute-start | bytes 786440 | tf_op jit(solution)/shard_map/while/body/eval_jaxpr/ppermute | solution.py:20
  563.1 11.2 %collective-permute-start = (bf16[64,1,8,128]{3,0,2,1:T(8,128)(2,1)S(1)}, bf16[64,1,8,128]{3,0,2,1:T(8,128)(2,1)S(1)}, u32[]{:S(2)}, u32[]{:S(2)}) collective-permute-start(bf16[64,1,8,128]{3,0,2,1:T(8,128)(2,1)S(1)} %copy.23), channel_id=1, source_target_pairs={{0,8},{8,16},{16,24},{24,32},{32,40},{40,48},{48,56},{56,64},{64,7... | collective-permute-start | bytes 393224 | tf_op jit(solution)/shard_map/while/body/eval_jaxpr/ppermute | solution.py:20
  582.6 11.3 %collective-permute-start.3 = (f32[1,8,64,128]{3,2,1,0:T(8,128)S(1)}, f32[1,8,64,128]{3,2,1,0:T(8,128)S(1)}, u32[]{:S(2)}, u32[]{:S(2)}) collective-permute-start(f32[1,8,64,128]{3,2,1,0:T(8,128)S(1)} %fusion.44), channel_id=1, source_target_pairs={{0,8},{8,16},{16,24},{24,32},{32,40},{40,48},{48,56},{56,64},{64,7... | collective-permute-start | bytes 786440 | tf_op jit(solution)/shard_map/while/body/eval_jaxpr/ppermute | solution.py:20
  582.7 11.2 %collective-permute-start = (bf16[64,1,8,128]{3,0,2,1:T(8,128)(2,1)S(1)}, bf16[64,1,8,128]{3,0,2,1:T(8,128)(2,1)S(1)}, u32[]{:S(2)}, u32[]{:S(2)}) collective-permute-start(bf16[64,1,8,128]{3,0,2,1:T(8,128)(2,1)S(1)} %copy.23), channel_id=1, source_target_pairs={{0,8},{8,16},{16,24},{24,32},{32,40},{40,48},{48,56},{56,64},{64,7... | collective-permute-start | bytes 393224 | tf_op jit(solution)/shard_map/while/body/eval_jaxpr/ppermute | solution.py:20
  602.2 11.3 %collective-permute-start.3 = (f32[1,8,64,128]{3,2,1,0:T(8,128)S(1)}, f32[1,8,64,128]{3,2,1,0:T(8,128)S(1)}, u32[]{:S(2)}, u32[]{:S(2)}) collective-permute-start(f32[1,8,64,128]{3,2,1,0:T(8,128)S(1)} %fusion.44), channel_id=1, source_target_pairs={{0,8},{8,16},{16,24},{24,32},{32,40},{40,48},{48,56},{56,64},{64,7... | collective-permute-start | bytes 786440 | tf_op jit(solution)/shard_map/while/body/eval_jaxpr/ppermute | solution.py:20
  602.3 11.2 %collective-permute-start = (bf16[64,1,8,128]{3,0,2,1:T(8,128)(2,1)S(1)}, bf16[64,1,8,128]{3,0,2,1:T(8,128)(2,1)S(1)}, u32[]{:S(2)}, u32[]{:S(2)}) collective-permute-start(bf16[64,1,8,128]{3,0,2,1:T(8,128)(2,1)S(1)} %copy.23), channel_id=1, source_target_pairs={{0,8},{8,16},{16,24},{24,32},{32,40},{40,48},{48,56},{56,64},{64,7... | collective-permute-start | bytes 393224 | tf_op jit(solution)/shard_map/while/body/eval_jaxpr/ppermute | solution.py:20
  621.7 11.3 %collective-permute-start.3 = (f32[1,8,64,128]{3,2,1,0:T(8,128)S(1)}, f32[1,8,64,128]{3,2,1,0:T(8,128)S(1)}, u32[]{:S(2)}, u32[]{:S(2)}) collective-permute-start(f32[1,8,64,128]{3,2,1,0:T(8,128)S(1)} %fusion.44), channel_id=1, source_target_pairs={{0,8},{8,16},{16,24},{24,32},{32,40},{40,48},{48,56},{56,64},{64,7... | collective-permute-start | bytes 786440 | tf_op jit(solution)/shard_map/while/body/eval_jaxpr/ppermute | solution.py:20
  621.8 11.2 %collective-permute-start = (bf16[64,1,8,128]{3,0,2,1:T(8,128)(2,1)S(1)}, bf16[64,1,8,128]{3,0,2,1:T(8,128)(2,1)S(1)}, u32[]{:S(2)}, u32[]{:S(2)}) collective-permute-start(bf16[64,1,8,128]{3,0,2,1:T(8,128)(2,1)S(1)} %copy.23), channel_id=1, source_target_pairs={{0,8},{8,16},{16,24},{24,32},{32,40},{40,48},{48,56},{56,64},{64,7... | collective-permute-start | bytes 393224 | tf_op jit(solution)/shard_map/while/body/eval_jaxpr/ppermute | solution.py:20
  641.3 11.3 %collective-permute-start.3 = (f32[1,8,64,128]{3,2,1,0:T(8,128)S(1)}, f32[1,8,64,128]{3,2,1,0:T(8,128)S(1)}, u32[]{:S(2)}, u32[]{:S(2)}) collective-permute-start(f32[1,8,64,128]{3,2,1,0:T(8,128)S(1)} %fusion.44), channel_id=1, source_target_pairs={{0,8},{8,16},{16,24},{24,32},{32,40},{40,48},{48,56},{56,64},{64,7... | collective-permute-start | bytes 786440 | tf_op jit(solution)/shard_map/while/body/eval_jaxpr/ppermute | solution.py:20
  641.4 11.2 %collective-permute-start = (bf16[64,1,8,128]{3,0,2,1:T(8,128)(2,1)S(1)}, bf16[64,1,8,128]{3,0,2,1:T(8,128)(2,1)S(1)}, u32[]{:S(2)}, u32[]{:S(2)}) collective-permute-start(bf16[64,1,8,128]{3,0,2,1:T(8,128)(2,1)S(1)} %copy.23), channel_id=1, source_target_pairs={{0,8},{8,16},{16,24},{24,32},{32,40},{40,48},{48,56},{56,64},{64,7... | collective-permute-start | bytes 393224 | tf_op jit(solution)/shard_map/while/body/eval_jaxpr/ppermute | solution.py:20
  (97 other events, 714.0 us)
Sparse Core Ops, SparseCore 0:
  658.7 36.9 reduce-scatter.1
where the time goes:
time: 708 us; the launch traced here: 703 us
  waiting for transfers between devices  372 us (53%)
  local copies, waits for them, and re-layouts  141 us (20%)
  matrix products  66.2 us (9%)
  other arithmetic  60.5 us (9%)
  starting transfers between devices  43.4 us (6%)
  between operations  13.5 us (2%)
    ppermute x128, waiting for transfers between devices, passed_along(): return lax.ppermute(value, axis, pairs)  335 us
    ppermute x128, starting transfers between devices, passed_along(): return lax.ppermute(value, axis, pairs)  43.4 us
    dot_general x32, matrix products, attend(): jnp.einsum('rkgd,nkd->kgrn', query_rows, key_rows, preferred_element_type...  40.4 us
    dynamic_slice x32, local copies, waits for them, and re-layouts, partial_for(): lax.dynamic_index_in_dim(turn_start, traj_index, 0, keepdims=False)  39.5 us
    dynamic_slice x32, local copies, waits for them, and re-layouts, partial_for(): lax.dynamic_index_in_dim(cache_lengths, traj_index, 0, keepdims=False)[0]  39.5 us
    reduce_scatter x1, waiting for transfers between devices, on_device(): lax.psum_scatter(jnp.dot(attended, out_weight, preferred_element_type=jnp...  37.1 us
    reshape x32, local copies, waits for them, and re-layouts, partial_for(): stored_values = lax.dynamic_index_in_dim(cache_values, traj_index, 0, kee...  30.3 us
    reshape x32, local copies, waits for them, and re-layouts, partial_for(): lax.dynamic_index_in_dim(cache_keys, traj_index, 0, keepdims=False)  30.3 us
  transfers between devices with their start and end apart: 129, of which 37 were waited for; matrix products, arithmetic and copies ran while one was open for 0% of the time, Pallas kernels for 0%

commit v1 on v0

v1 whole, which is shorter than its diff:
```python
import math

import jax
import jax.numpy as jnp
from jax import lax
from jax.experimental import pallas as pl
from jax.experimental.pallas import tpu as pltpu
from jax.sharding import PartitionSpec as P

HD = 128
GROUP = 8
NY = 4
NZ = 8
NTP = 8
SHARD = 768
HALF = SHARD // 2
HOME_ROWS = 64
QC = GROUP * HOME_ROWS
N_HOME = 4
OUT = 4096
VROWS = HD + 16
MASKED = -1e30
EXP2_SCALE = math.log2(math.e) / math.sqrt(HD)
DY = (0, 1, 3, 2)
N_COL = 2
COL = OUT // N_COL
MESH = pl.DeviceIdType.MESH


def kernel(
    q_ref, nk_ref, nv_ref, ck_ref, cv_ref, len_ref, start_ref, w_ref, out_ref,
    qst, qbuf, kbuf, vbuf, kp, vt, lst, lbuf, nkbuf, nvbuf, vtn, acc, mx,
    ost, sst, obuf, sbuf, att, wbuf, pst, rbuf,
    w_sem, kv_send, kv_recv, l_send, l_recv, q_send, q_recv,
    n_send, n_recv, o_send, o_recv, s_send, s_recv, p_send, p_recv,
):
    ctx = lax.axis_index("ctx")
    tp = lax.axis_index("tp")
    y = ctx // NZ
    z = ctx % NZ
    par = z % 2
    held = 2 * y + par
    home_par = z // 4
    home_slot = z % 4

    def at(row, col):
        return {"ctx": row * NZ + col, "tp": tp}

    def row_of(oi):
        return (y + DY[oi]) % NY

    barrier = pltpu.get_barrier_semaphore()
    n_peers = 0
    for dy in range(NY):
        for dz in range(NZ):
            if (dy == 0 and dz != 0) or (dy != 0 and dz in (0, 1, NZ - 1)):
                pl.semaphore_signal(
                    barrier, inc=1, device_id=at((y + dy) % NY, (z + dz) % NZ), device_id_type=MESH
                )
                n_peers += 1
    for d in range(1, NTP):
        pl.semaphore_signal(
            barrier, inc=1, device_id={"ctx": ctx, "tp": (tp + d) % NTP}, device_id_type=MESH
        )
        n_peers += 1

    w_copy = pltpu.make_async_copy(w_ref, wbuf, w_sem)
    own = []
    for h in range(2):
        rows = pl.ds(h * HALF, HALF)
        for kv, (src, dst) in enumerate(((ck_ref, kbuf), (cv_ref, vbuf))):
            own.append(
                pltpu.make_async_copy(
                    src.at[held, rows], dst.at[0, rows], kv_recv.at[0, h, kv]
                )
            )
    for copy in own:
        copy.start()
    w_copy.start()
    for g in range(GROUP):
        qst[pl.ds(g * HOME_ROWS, HOME_ROWS), :] = q_ref[:, pl.ds(g * HD, HD)]
    for oi in range(NY):
        row = row_of(oi)
        lst[oi, 0] = jnp.full((8, 128), len_ref[2 * row + par, 0], jnp.int32)
        lst[oi, 1] = jnp.full((8, 128), len_ref[2 * row + 1 - par, 0], jnp.int32)
    lbuf[0, 0] = lst[0, 0]

    pl.semaphore_wait(barrier, n_peers)

    def remote(src, dst, send, recv, device):
        return pltpu.make_async_remote_copy(
            src_ref=src, dst_ref=dst, send_sem=send, recv_sem=recv,
            device_id=device, device_id_type=MESH,
        )

    def q_copy(i):
        return remote(
            qst, qbuf.at[home_slot], q_send.at[i], q_recv.at[home_slot], at(y, 2 * i + home_par)
        )

    def q_local():
        return pltpu.make_async_copy(qst, qbuf.at[home_slot], q_recv.at[home_slot])

    for i in range(N_HOME):
        target = 2 * i + home_par

        @pl.when(target != z)
        def _():
            q_copy(i).start()

        @pl.when(target == z)
        def _():
            q_local().start()

    new_target = 2 * home_slot + home_par

    def n_copy(kv):
        return remote(
            (nk_ref, nv_ref)[kv], (nkbuf, nvbuf)[kv], n_send.at[kv], n_recv.at[kv], at(y, new_target)
        )

    def n_local(kv):
        return pltpu.make_async_copy((nk_ref, nv_ref)[kv], (nkbuf, nvbuf)[kv], n_recv.at[kv])

    for kv in range(2):

        @pl.when(new_target != z)
        def _():
            n_copy(kv).start()

        @pl.when(new_target == z)
        def _():
            n_local(kv).start()

    kv_copies = []
    l_copies = []
    for oi in range(NY):
        row = row_of(oi)
        for cross in range(2):
            if oi == 0 and cross == 0:
                continue
            traj = 2 * row + (1 - par if cross else par)
            for h in range(2):
                dz = 0 if not cross else (1 if h == 0 else NZ - 1)
                device = at(row, (z + dz) % NZ)
                if cross or h == 0:
                    slot = 0 if not cross else 1 + h
                    l_copies.append(
                        remote(
                            lst.at[oi, cross], lbuf.at[oi, slot],
                            l_send.at[oi, slot], l_recv.at[oi, slot], device,
                        )
                    )
                rows = pl.ds(h * HALF, HALF)
                for kv, (src, dst) in enumerate(((ck_ref, kbuf), (cv_ref, vbuf))):
                    b = 2 * oi + cross
                    kv_copies.append(
                        remote(
                            src.at[traj, rows], dst.at[b, rows],
                            kv_send.at[b, h, kv], kv_recv.at[b, h, kv], device,
                        )
                    )
    for copy in l_copies:
        copy.start()
    for copy in kv_copies:
        copy.start()

    acc[...] = jnp.zeros_like(acc)
    mx[...] = jnp.full_like(mx, MASKED)
    sst[...] = jnp.zeros_like(sst)

    for j in range(N_HOME):
        pltpu.make_async_copy(qst, qbuf.at[j], q_recv.at[j]).wait()

    def update(j, s, vt_rows):
        old = mx[j, 0:1, :]
        new = jnp.maximum(old, jnp.max(s, axis=0, keepdims=True))
        p = jnp.exp2((s - new) * EXP2_SCALE).astype(jnp.bfloat16)
        fade = jnp.exp2((old - new) * EXP2_SCALE)
        part = jnp.dot(vt_rows, p, preferred_element_type=jnp.float32)
        acc[j] = acc[j] * fade + part
        mx[j, 0:1, :] = new

    def scores(keys, j):
        return lax.dot_general(
            keys, qbuf[j], (((1,), (1,)), ((), ())), preferred_element_type=jnp.float32
        )

    position = lax.broadcasted_iota(jnp.int32, (HALF, HD), 0)
    lane_position = lax.broadcasted_iota(jnp.int32, (16, HD), 1)
    first_row = lax.broadcasted_iota(jnp.int32, (16, HD), 0) == 0

    def block(b, carry):
        oi = b // 2
        cross = b % 2
        for h in range(2):
            rows = pl.ds(h * HALF, HALF)
            slot = cross * (1 + h)

            if h == 0:

                @pl.when(b > 0)
                def _():
                    pltpu.make_async_copy(
                        lst.at[0, 0], lbuf.at[oi, slot], l_recv.at[oi, slot]
                    ).wait()

            else:

                @pl.when(cross == 1)
                def _():
                    pltpu.make_async_copy(
                        lst.at[0, 0], lbuf.at[oi, slot], l_recv.at[oi, slot]
                    ).wait()

            pltpu.make_async_copy(
                ck_ref.at[0, rows], kbuf.at[b, rows], kv_recv.at[b, h, 0]
            ).wait()
            pltpu.make_async_copy(
                cv_ref.at[0, rows], vbuf.at[b, rows], kv_recv.at[b, h, 1]
            ).wait()
        for h in range(2):
            rows = pl.ds(h * HALF, HALF)
            fill = lbuf[oi, cross * (1 + h)]
            ok = position + h * HALF < fill[0:1, :]
            spare = kbuf[0, 0:16, :].astype(jnp.float32)[0:1, :]
            keys = kbuf[b, rows, :].astype(jnp.float32)
            kp[rows, :] = jnp.where(ok, keys, spare).astype(jnp.bfloat16)
            values = jnp.where(ok, vbuf[b, rows, :].astype(jnp.float32), 0.0)
            vt[0:HD, rows] = values.T.astype(jnp.bfloat16)
            for g in range(HALF // HD):
                first = h * HALF + g * HD
                counted = first_row & (lane_position + first < fill[0:1, :])
                vt[HD:VROWS, pl.ds(first, HD)] = jnp.where(counted, 1.0, 0.0).astype(jnp.bfloat16)

        def chunk(j, carry):
            update(j, scores(kp[...], j), vt[...])
            return carry

        return lax.fori_loop(0, N_HOME, chunk, carry)

    lax.fori_loop(0, 1, block, 0)

    for kv in range(2):
        pltpu.make_async_copy(
            (nk_ref, nv_ref)[kv], (nkbuf, nvbuf)[kv], n_recv.at[kv]
        ).wait()
    vtn[0:HD, :] = nvbuf[...].astype(jnp.float32).T.astype(jnp.bfloat16)
    ones = lax.broadcasted_iota(jnp.int32, (16, HOME_ROWS), 0) == 0
    vtn[HD:VROWS, :] = jnp.where(ones, 1.0, 0.0).astype(jnp.bfloat16)
    key_pos = (z // 2) * HOME_ROWS + lax.broadcasted_iota(jnp.int32, (HOME_ROWS, QC), 0)
    row_pos = lax.broadcasted_iota(jnp.int32, (HOME_ROWS, QC), 1) % HOME_ROWS
    begun = key_pos >= start_ref[held]

    def new_chunk(j, carry):
        ok = begun & (key_pos <= row_pos + j * HOME_ROWS)
        update(j, jnp.where(ok, scores(nkbuf[...], j), MASKED), vtn[...])
        return carry

    lax.fori_loop(0, N_HOME, new_chunk, 0)

    lax.fori_loop(1, 2 * NY, block, 0)

    def o_copy(j):
        device = at(y, 4 * par + j)
        return (
            remote(ost.at[j], obuf.at[z // 2], o_send.at[j], o_recv.at[z // 2], device),
            remote(sst.at[j], sbuf.at[z // 2], s_send.at[j], s_recv.at[z // 2], device),
        )

    def o_local(j):
        return (
            pltpu.make_async_copy(ost.at[j], obuf.at[z // 2], o_recv.at[z // 2]),
            pltpu.make_async_copy(sst.at[j], sbuf.at[z // 2], s_recv.at[z // 2]),
        )

    for j in range(N_HOME):
        ost[j] = acc[j, 0:HD, :].astype(jnp.bfloat16)
        sst[j, 0:1, :] = mx[j, 0:1, :]
        sst[j, 1:2, :] = acc[j, HD : HD + 1, :]

        @pl.when(4 * par + j != z)
        def _():
            for copy in o_copy(j):
                copy.start()

        @pl.when(4 * par + j == z)
        def _():
            for copy in o_local(j):
                copy.start()

    w_copy.wait()
    for i in range(N_HOME):
        pltpu.make_async_copy(ost.at[0], obuf.at[i], o_recv.at[i]).wait()
        pltpu.make_async_copy(sst.at[0], sbuf.at[i], s_recv.at[i]).wait()

    top = sbuf[0, 0:1, :]
    for i in range(1, N_HOME):
        top = jnp.maximum(top, sbuf[i, 0:1, :])
    total = jnp.zeros((1, QC), jnp.float32)
    summed = jnp.zeros((HD, QC), jnp.float32)
    for i in range(N_HOME):
        factor = jnp.exp2((sbuf[i, 0:1, :] - top) * EXP2_SCALE)
        total = total + factor * sbuf[i, 1:2, :]
        summed = summed + factor * obuf[i].astype(jnp.float32)
    attended = (summed / total).T
    for g in range(GROUP):
        att[:, pl.ds(g * HD, HD)] = attended[g * HOME_ROWS : (g + 1) * HOME_ROWS].astype(jnp.bfloat16)

    def p_copy(c, d):
        to = (tp + d) % NTP
        return remote(
            pst.at[c, to], rbuf.at[c, tp], p_send.at[c, d], p_recv.at[c, tp], {"ctx": ctx, "tp": to}
        )

    for c in range(N_COL):
        for g in range(2):
            half = c * COL + g * (COL // 2)
            prod = jnp.dot(
                att[...], wbuf[:, pl.ds(half, COL // 2)], preferred_element_type=jnp.float32
            )
            for t in range(NTP):
                pst[c, t, pl.ds(g * 8, 8), :] = prod[t * 8 : (t + 1) * 8, :].astype(jnp.bfloat16)
        for d in range(1, NTP):
            p_copy(c, d).start()

    for c in range(N_COL):
        sums = pst[c, tp].astype(jnp.float32)
        for d in range(1, NTP):
            source = (tp + d) % NTP
            pltpu.make_async_copy(pst.at[c, 0], rbuf.at[c, source], p_recv.at[c, source]).wait()
            sums = sums + rbuf[c, source].astype(jnp.float32)
        for g in range(2):
            out_ref[:, pl.ds(c * COL + g * (COL // 2), COL // 2)] = sums[g * 8 : (g + 1) * 8].astype(
                jnp.bfloat16
            )

    for i in range(N_HOME):

        @pl.when(2 * i + home_par != z)
        def _():
            q_copy(i).wait_send()

    for kv in range(2):

        @pl.when(new_target != z)
        def _():
            n_copy(kv).wait_send()

    for copy in l_copies + kv_copies:
        copy.wait_send()
    for j in range(N_HOME):

        @pl.when(4 * par + j != z)
        def _():
            for copy in o_copy(j):
                copy.wait_send()

    for c in range(N_COL):
        for d in range(1, NTP):
            p_copy(c, d).wait_send()


def on_device(queries, new_keys, new_values, cache_keys, cache_values, lengths, turn_start, out_weight):
    vmem = pl.BlockSpec(memory_space=pltpu.VMEM)
    smem = pl.BlockSpec(memory_space=pltpu.SMEM)
    hbm = pl.BlockSpec(memory_space=pl.ANY)
    bf16, f32, i32 = jnp.bfloat16, jnp.float32, jnp.int32
    dma = pltpu.SemaphoreType.DMA
    return pl.pallas_call(
        kernel,
        out_shape=jax.ShapeDtypeStruct((HOME_ROWS // NTP, OUT), bf16),
        in_specs=[vmem, vmem, vmem, hbm, hbm, smem, smem, hbm],
        out_specs=vmem,
        scratch_shapes=[
            pltpu.VMEM((QC, HD), bf16),
            pltpu.VMEM((N_HOME, QC, HD), bf16),
            pltpu.VMEM((2 * NY, SHARD, HD), bf16),
            pltpu.VMEM((2 * NY, SHARD, HD), bf16),
            pltpu.VMEM((SHARD, HD), bf16),
            pltpu.VMEM((VROWS, SHARD), bf16),
            pltpu.VMEM((NY, 2, 8, 128), i32),
            pltpu.VMEM((NY, 3, 8, 128), i32),
            pltpu.VMEM((HOME_ROWS, HD), bf16),
            pltpu.VMEM((HOME_ROWS, HD), bf16),
            pltpu.VMEM((VROWS, HOME_ROWS), bf16),
            pltpu.VMEM((N_HOME, VROWS, QC), f32),
            pltpu.VMEM((N_HOME, 8, QC), f32),
            pltpu.VMEM((N_HOME, HD, QC), bf16),
            pltpu.VMEM((N_HOME, 8, QC), f32),
            pltpu.VMEM((N_HOME, HD, QC), bf16),
            pltpu.VMEM((N_HOME, 8, QC), f32),
            pltpu.VMEM((HOME_ROWS, GROUP * HD), bf16),
            pltpu.VMEM((GROUP * HD, OUT), bf16),
            pltpu.VMEM((N_COL, NTP, 16, COL // 2), bf16),
            pltpu.VMEM((N_COL, NTP, 16, COL // 2), bf16),
            dma,
            dma((2 * NY, 2, 2)),
            dma((2 * NY, 2, 2)),
            dma((NY, 3)),
            dma((NY, 3)),
            dma((N_HOME,)),
            dma((N_HOME,)),
            dma((2,)),
            dma((2,)),
            dma((N_HOME,)),
            dma((N_HOME,)),
            dma((N_HOME,)),
            dma((N_HOME,)),
            dma((N_COL, NTP)),
            dma((N_COL, NTP)),
        ],
        compiler_params=pltpu.CompilerParams(
            collective_id=0, has_side_effects=True, vmem_limit_bytes=48 << 20
        ),
        name="attend_project",
    )(queries, new_keys, new_values, cache_keys, cache_values, lengths, turn_start, out_weight)


def solution(mesh):
    in_specs = (
        P("ctx", "tp"),
        P("ctx", "tp"),
        P("ctx", "tp"),
        P(None, "ctx", "tp"),
        P(None, "ctx", "tp"),
        P(None, "ctx"),
        P(),
        P("tp", None),
    )
    return jax.shard_map(
        on_device, mesh=mesh, in_specs=in_specs, out_specs=P(("ctx", "tp"), None), check_vma=False
    )
```

time: 708 us -> 92.5 us (0.13)
  waiting for transfers between devices: 372 us -> 0 us
  local copies, waits for them, and re-layouts: 141 us -> 7.17 us
  Pallas kernels: 0 us -> 84.7 us
  matrix products: 66.2 us -> 0 us
  other arithmetic: 60.5 us -> 0 us
  starting transfers between devices: 43.4 us -> 0 us
  between operations: 13.5 us -> 0.02 us
    ppermute x128 -> x0, waiting for transfers between devices: 335 us -> none  [passed_along(): return lax.ppermute(value, axis, pairs)]
    pallas_call x0 -> x1, Pallas kernels: none -> 84.7 us  [on_device(): pl.pallas_call(kernel, out_shape=jax.ShapeDtypeStruct((HOME_ROWS // NTP,...]
    dynamic_slice x64 -> x0, local copies, waits for them, and re-layouts: 79.1 us -> none  [the longest x32 39.5 us: partial_for(): lax.dynamic_index_in_dim(turn_start, traj_index, 0, keepdims=False)]
    dot_general x65 -> x0, matrix products: 66.2 us -> none  [the longest x32 40.4 us: attend(): jnp.einsum('rkgd,nkd->kgrn', query_rows, key_rows, preferred_element_type...]
    reshape x64 -> x0, local copies, waits for them, and re-layouts: 60.6 us -> none  [the longest x32 30.3 us: partial_for(): stored_values = lax.dynamic_index_in_dim(cache_values, traj_index, 0, kee...]
    ppermute x128 -> x0, starting transfers between devices: 43.4 us -> none  [passed_along(): return lax.ppermute(value, axis, pairs)]
    reduce_scatter x1 -> x0, waiting for transfers between devices: 37.1 us -> none  [on_device(): lax.psum_scatter(jnp.dot(attended, out_weight, preferred_element_type=jnp...]
    reduce_sum x32 -> x0, other arithmetic: 19.9 us -> none  [attend(): totals = jnp.sum(weights, axis=-1)]
  transfers between devices with their start and end apart: 129 -> 0, of which waited for: 37 -> 0; matrix products, arithmetic and copies ran while one was open for 0% -> 0% of each run, Pallas kernels for 0% -> 0%
where the time goes in v1:
time: 92.5 us; the launch traced here: 91.9 us
  Pallas kernels  84.7 us (92%)
  local copies, waits for them, and re-layouts  7.17 us (8%)
    pallas_call x1, Pallas kernels, on_device(): pl.pallas_call(kernel, out_shape=jax.ShapeDtypeStruct((HOME_ROWS // NTP,...  84.7 us
    unnamed x14, local copies, waits for them, and re-layouts  7.17 us

profile of v1, /device:TPU:64, one launch (start us, length us, event | category | flops | bytes accessed | tf_op | source)
XLA Modules:
  0.0 91.9 jit_solution(13157483263547219519)
XLA Ops:
  0.0 0.7 copy.9.len_ref
  0.7 0.0 copy-start
  0.7 1.4 %copy-done = bf16[8,768,128]{2,1,0:T(8,128)(2,1)S(1)} copy-done((bf16[8,768,128]{2,1,0:T(8,128)(2,1)S(1)}, bf16[8,768,128]{2,1,0:T(8,128)(2,1)}, u32[]{:S(2)}) %copy-start) | copy-done | bytes 1572888
  2.1 0.0 copy-start.1
  2.1 1.4 %copy-done.1 = bf16[8,768,128]{2,1,0:T(8,128)(2,1)S(1)} copy-done((bf16[8,768,128]{2,1,0:T(8,128)(2,1)S(1)}, bf16[8,768,128]{2,1,0:T(8,128)(2,1)}, u32[]{:S(2)}) %copy-start.1) | copy-done | bytes 1572888
  3.5 0.0 copy-start.2
  3.5 0.9 copy-done.2
  4.5 0.0 copy-start.3
  4.5 0.7 copy-done.3
  5.2 0.0 copy-start.4
  5.2 0.7 copy-done.4
  5.9 0.0 copy-start.5
  5.9 0.7 copy-done.5
  6.5 84.7 %attend_project.1 = bf16[8,4096]{1,0:T(8,128)(2,1)S(1)} custom-call(bf16[64,1024]{1,0:T(8,128)(2,1)S(1)} %copy-done.2, bf16[64,128]{1,0:T(8,128)(2,1)S(1)} %copy-done.3, bf16[64,128]{1,0:T(8,128)(2,1)S(1)} %copy-done.4, bf16[8,768,128]{2,1,0:T(8,128)(2,1)S(1)} %copy-done, bf16[8,768,128]{2,1,0:T(8,128)(2,1)S(1)} %copy-done.1, s32[8,1]{1,0:T(8,128)S(1)} %copy.9.len_ref, ...), custom_call_target="tpu_custom_call" | custom-call | tf_op jit(solution)/shard_map/attend_project/pallas_call | solution.py:370
  91.3 0.6 copy.11
Async XLA Ops:
  0.7 1.4 %copy-start = (bf16[8,768,128]{2,1,0:T(8,128)(2,1)S(1)}, bf16[8,768,128]{2,1,0:T(8,128)(2,1)}, u32[]{:S(2)}) copy-start(bf16[8,768,128]{2,1,0:T(8,128)(2,1)} %ck_ref.1) | copy-start | bytes 4718596
  2.1 1.4 %copy-start.1 = (bf16[8,768,128]{2,1,0:T(8,128)(2,1)S(1)}, bf16[8,768,128]{2,1,0:T(8,128)(2,1)}, u32[]{:S(2)}) copy-start(bf16[8,768,128]{2,1,0:T(8,128)(2,1)} %cv_ref.1) | copy-start | bytes 4718596
  3.5 0.9 copy-start.2
  4.5 0.7 copy-start.3
  5.2 0.7 copy-start.4
  5.9 0.7 copy-start.5

commit v2 on v1

v2 whole, which is shorter than its diff:
```python
import math

import jax
import jax.numpy as jnp
from jax import lax
from jax.experimental import pallas as pl
from jax.experimental.pallas import tpu as pltpu
from jax.sharding import PartitionSpec as P

HD = 128
GROUP = 8
NY = 4
NZ = 8
NTP = 8
NX = 4
SHARD = 768
HALF = SHARD // 2
HOME_ROWS = 64
QC = GROUP * HOME_ROWS
N_HOME = 4
GL = QC // 2
OUT = 4096
VROWS = HD + 16
MASKED = -1e30
EXP2_SCALE = math.log2(math.e) / math.sqrt(HD)
DY = (0, 1, 3, 2)
N_COL = 4
COL = OUT // N_COL
MESH = pl.DeviceIdType.MESH


def kernel(
    q_hbm, nk_ref, nv_ref, ck_ref, cv_ref, len_hbm, start_hbm, w_ref, out_ref,
    q_ref, len_ref, start_ref, qst, qbuf, kbuf, vbuf, kp, vt, sa, sb, lst, lbuf, nkbuf, nvbuf, vtn, acc, mx,
    ost, sst, obuf, sbuf, att, proj, wbuf, pst, cbuf, xst, rbuf,
    in_sem, w_sem, kv_send, kv_recv, l_send, l_recv, q_send, q_recv,
    n_send, n_recv, o_send, o_recv, s_send, s_recv, c_send, c_recv, p_send, p_recv,
):
    ctx = lax.axis_index("ctx")
    tp = lax.axis_index("tp")
    y = ctx // NZ
    z = ctx % NZ
    x = tp // 2
    core = tp % 2
    par = z % 2
    held = 2 * y + par
    home_par = z // 4
    home_slot = z % 4

    def at(row, col):
        return {"ctx": row * NZ + col, "tp": tp}

    sibling = {"ctx": ctx, "tp": tp // 2 * 2 + 1 - core}

    def across(d):
        return {"ctx": ctx, "tp": (x + d) % NX * 2 + core}

    def row_of(oi):
        return (y + DY[oi]) % NY

    inputs = [
        pltpu.make_async_copy(src, dst, in_sem.at[i])
        for i, (src, dst) in enumerate(((q_hbm, q_ref), (len_hbm, len_ref), (start_hbm, start_ref)))
    ]
    for copy in inputs:
        copy.start()

    barrier = pltpu.get_barrier_semaphore()
    n_peers = 0
    for dy in range(NY):
        for dz in range(NZ):
            if (dy == 0 and dz != 0) or (dy != 0 and dz in (0, 1, NZ - 1)):
                pl.semaphore_signal(
                    barrier, inc=1, device_id=at((y + dy) % NY, (z + dz) % NZ), device_id_type=MESH
                )
                n_peers += 1
    for peer in [sibling] + [across(d) for d in range(1, NX)]:
        pl.semaphore_signal(barrier, inc=1, device_id=peer, device_id_type=MESH)
        n_peers += 1

    w_copy = pltpu.make_async_copy(w_ref, wbuf, w_sem)
    own = []
    for h in range(2):
        rows = pl.ds(h * HALF, HALF)
        for kv, (src, dst) in enumerate(((ck_ref, kbuf), (cv_ref, vbuf))):
            own.append(
                pltpu.make_async_copy(
                    src.at[held, rows], dst.at[0, rows], kv_recv.at[0, h, kv]
                )
            )
    for copy in own:
        copy.start()
    w_copy.start()
    for copy in inputs:
        copy.wait()
    for g in range(GROUP):
        qst[pl.ds(g * HOME_ROWS, HOME_ROWS), :] = q_ref[:, pl.ds(g * HD, HD)]
    for oi in range(NY):
        row = row_of(oi)
        lst[oi, 0] = jnp.full((8, 128), len_ref[0, 2 * row + par], jnp.int32)
        lst[oi, 1] = jnp.full((8, 128), len_ref[0, 2 * row + 1 - par], jnp.int32)
    lbuf[0, 0] = lst[0, 0]

    pl.semaphore_wait(barrier, n_peers)

    def remote(src, dst, send, recv, device):
        return pltpu.make_async_remote_copy(
            src_ref=src, dst_ref=dst, send_sem=send, recv_sem=recv,
            device_id=device, device_id_type=MESH,
        )

    kv_first = []
    kv_copies = []
    l_copies = []
    for oi in range(NY):
        row = row_of(oi)
        for cross in range(2):
            if oi == 0 and cross == 0:
                continue
            traj = 2 * row + (1 - par if cross else par)
            for h in range(2):
                dz = 0 if not cross else (1 if h == 0 else NZ - 1)
                device = at(row, (z + dz) % NZ)
                if cross or h == 0:
                    slot = 0 if not cross else 1 + h
                    l_copies.append(
                        remote(
                            lst.at[oi, cross], lbuf.at[oi, slot],
                            l_send.at[oi, slot], l_recv.at[oi, slot], device,
                        )
                    )
                rows = pl.ds(h * HALF, HALF)
                for kv, (src, dst) in enumerate(((ck_ref, kbuf), (cv_ref, vbuf))):
                    b = 2 * oi + cross
                    copy = remote(
                        src.at[traj, rows], dst.at[b, rows],
                        kv_send.at[b, h, kv], kv_recv.at[b, h, kv], device,
                    )
                    (kv_first if oi in (1, 2) and not cross else kv_copies).append(copy)
    for copy in kv_first:
        copy.start()

    def q_copy(i):
        return remote(
            qst, qbuf.at[home_slot], q_send.at[i], q_recv.at[home_slot], at(y, 2 * i + home_par)
        )

    def q_local():
        return pltpu.make_async_copy(qst, qbuf.at[home_slot], q_recv.at[home_slot])

    for i in range(N_HOME):
        target = 2 * i + home_par

        @pl.when(target != z)
        def _():
            q_copy(i).start()

        @pl.when(target == z)
        def _():
            q_local().start()

    new_target = 2 * home_slot + home_par

    def n_copy(kv):
        return remote(
            (nk_ref, nv_ref)[kv], (nkbuf, nvbuf)[kv], n_send.at[kv], n_recv.at[kv], at(y, new_target)
        )

    def n_local(kv):
        return pltpu.make_async_copy((nk_ref, nv_ref)[kv], (nkbuf, nvbuf)[kv], n_recv.at[kv])

    for kv in range(2):

        @pl.when(new_target != z)
        def _():
            n_copy(kv).start()

        @pl.when(new_target == z)
        def _():
            n_local(kv).start()

    for copy in l_copies + kv_copies:
        copy.start()

    acc[...] = jnp.zeros_like(acc)
    mx[...] = jnp.full_like(mx, MASKED)
    sst[...] = jnp.zeros_like(sst)

    for j in range(N_HOME):
        pltpu.make_async_copy(qst, qbuf.at[j], q_recv.at[j]).wait()

    def scores(keys, j, held_scores):
        s = lax.dot_general(
            keys, qbuf[j], (((1,), (1,)), ((), ())), preferred_element_type=jnp.float32
        )
        held_scores[...] = s
        old = mx[j, 0:1, :]
        new = jnp.maximum(old, jnp.max(s, axis=0, keepdims=True))
        mx[j, 0:1, :] = new
        return old, new

    def update(j, s, old, new, vt_rows):
        p = jnp.exp2((s - new) * EXP2_SCALE).astype(jnp.bfloat16)
        fade = jnp.exp2((old - new) * EXP2_SCALE)
        part = jnp.dot(vt_rows, p, preferred_element_type=jnp.float32)
        acc[j] = acc[j] * fade + part

    def sweep(first, count, done=None):
        rows = pl.ds(first, count)
        buffers = (sa.at[pl.ds(0, count)], sb.at[pl.ds(0, count)])
        state = scores(kp[rows, :], 0, buffers[0])
        for j in range(N_HOME):
            ahead = scores(kp[rows, :], j + 1, buffers[(j + 1) % 2]) if j + 1 < N_HOME else None
            update(j, buffers[j % 2][...], *state, vt[:, rows])
            if done is not None:
                done(j)
            state = ahead

    position = lax.broadcasted_iota(jnp.int32, (HALF, HD), 0)
    lane_position = lax.broadcasted_iota(jnp.int32, (16, HD), 1)
    first_row = lax.broadcasted_iota(jnp.int32, (16, HD), 0) == 0

    def arrive(b, at_key):
        oi = b // 2
        cross = b % 2
        for h in range(2):
            rows = pl.ds(h * HALF, HALF)
            slot = cross * (1 + h)
            if b > 0 and (cross or h == 0):
                pltpu.make_async_copy(lst.at[0, 0], lbuf.at[oi, slot], l_recv.at[oi, slot]).wait()
            pltpu.make_async_copy(ck_ref.at[0, rows], kbuf.at[b, rows], kv_recv.at[b, h, 0]).wait()
            pltpu.make_async_copy(cv_ref.at[0, rows], vbuf.at[b, rows], kv_recv.at[b, h, 1]).wait()
        spare = kbuf[0, 0:16, :].astype(jnp.float32)[0:1, :]
        for h in range(2):
            rows = pl.ds(h * HALF, HALF)
            put = pl.ds(at_key + h * HALF, HALF)
            fill = lbuf[oi, cross * (1 + h)]
            ok = position + h * HALF < fill[0:1, :]
            keys = kbuf[b, rows, :].astype(jnp.float32)
            kp[put, :] = jnp.where(ok, keys, spare).astype(jnp.bfloat16)
            values = jnp.where(ok, vbuf[b, rows, :].astype(jnp.float32), 0.0)
            vt[0:HD, put] = values.T.astype(jnp.bfloat16)
            for g in range(HALF // HD):
                first = h * HALF + g * HD
                counted = first_row & (lane_position + first < fill[0:1, :])
                vt[HD:VROWS, pl.ds(at_key + first, HD)] = jnp.where(counted, 1.0, 0.0).astype(
                    jnp.bfloat16
                )

    for oi in range(NY - 1):
        arrive(2 * oi, 0)
        arrive(2 * oi + 1, SHARD)
        sweep(0, 2 * SHARD)

    for kv in range(2):
        pltpu.make_async_copy(
            (nk_ref, nv_ref)[kv], (nkbuf, nvbuf)[kv], n_recv.at[kv]
        ).wait()
    vtn[0:HD, :] = nvbuf[...].astype(jnp.float32).T.astype(jnp.bfloat16)
    ones = lax.broadcasted_iota(jnp.int32, (16, HOME_ROWS), 0) == 0
    vtn[HD:VROWS, :] = jnp.where(ones, 1.0, 0.0).astype(jnp.bfloat16)
    key_pos = (z // 2) * HOME_ROWS + lax.broadcasted_iota(jnp.int32, (HOME_ROWS, QC), 0)
    row_pos = lax.broadcasted_iota(jnp.int32, (HOME_ROWS, QC), 1) % HOME_ROWS
    begun = key_pos >= start_ref[held]
    for j in range(N_HOME):
        s = lax.dot_general(
            nkbuf[...], qbuf[j], (((1,), (1,)), ((), ())), preferred_element_type=jnp.float32
        )
        s = jnp.where(begun & (key_pos <= row_pos + j * HOME_ROWS), s, MASKED)
        old = mx[j, 0:1, :]
        new = jnp.maximum(old, jnp.max(s, axis=0, keepdims=True))
        mx[j, 0:1, :] = new
        update(j, s, old, new, vtn[...])

    arrive(2 * NY - 2, 0)
    sweep(0, SHARD)
    arrive(2 * NY - 1, 0)

    def o_pairs(j, g):
        me = z // 2
        return (
            (ost.at[j, g], obuf.at[me, g], o_send.at[j, g], o_recv.at[me, g]),
            (sst.at[j, g], sbuf.at[me, g], s_send.at[j, g], s_recv.at[me, g]),
        )

    def send_partial(j, g):
        for i in range(GL // 128):
            lanes = pl.ds(g * GL + i * 128, 128)
            sst[j, g, i : i + 1, :] = mx[j, 0:1, lanes]
            sst[j, g, 4 + i : 5 + i, :] = acc[j, HD : HD + 1, lanes]
        ost[j, g] = acc[j, 0:HD, pl.ds(g * GL, GL)].astype(jnp.bfloat16)

        @pl.when(4 * par + j != z)
        def _():
            for src, dst, send, recv in o_pairs(j, g):
                remote(src, dst, send, recv, at(y, 4 * par + j)).start()

        @pl.when(4 * par + j == z)
        def _():
            for src, dst, send, recv in o_pairs(j, g):
                pltpu.make_async_copy(src, dst, recv).start()

    sweep(0, SHARD, lambda j: send_partial(j, 0))
    for j in range(N_HOME):
        send_partial(j, 1)

    w_copy.wait()

    def attend_group(g):
        for i in range(N_HOME):
            pltpu.make_async_copy(ost.at[0, g], obuf.at[i, g], o_recv.at[i, g]).wait()
            pltpu.make_async_copy(sst.at[0, g], sbuf.at[i, g], s_recv.at[i, g]).wait()

        def stat(i, first):
            rows = [sbuf[i, g, first + n : first + n + 1, :] for n in range(GL // 128)]
            return jnp.concatenate(rows, axis=1)

        highest = [stat(i, 0) for i in range(N_HOME)]
        top = highest[0]
        for i in range(1, N_HOME):
            top = jnp.maximum(top, highest[i])
        total = jnp.zeros((1, GL), jnp.float32)
        summed = jnp.zeros((HD, GL), jnp.float32)
        for i in range(N_HOME):
            factor = jnp.exp2((highest[i] - top) * EXP2_SCALE)
            total = total + factor * stat(i, 4)
            summed = summed + factor * obuf[i, g].astype(jnp.float32)
        attended = (summed / total).T
        for n in range(GL // HOME_ROWS):
            att[g, :, pl.ds(n * HD, HD)] = attended[n * HOME_ROWS : (n + 1) * HOME_ROWS].astype(
                jnp.bfloat16
            )

    depth = GROUP * HD // 2
    attend_group(0)
    for c in range(2 * N_COL):
        cols = pl.ds(c * (COL // 2), COL // 2)
        proj[:, cols] = jnp.dot(
            att[0], wbuf[pl.ds(0, depth), cols], preferred_element_type=jnp.float32
        )
    attend_group(1)

    def c_copy(c):
        return remote(
            pst.at[c, 1 - core], cbuf.at[c], c_send.at[c], c_recv.at[c], sibling
        )

    def p_copy(c, d):
        to = (x + d) % NX
        return remote(
            xst.at[c, to], rbuf.at[c, x], p_send.at[c, d], p_recv.at[c, x], across(d)
        )

    def project(c):
        for g in range(2):
            cols = pl.ds(c * COL + g * (COL // 2), COL // 2)
            prod = proj[:, cols] + jnp.dot(
                att[1], wbuf[pl.ds(depth, depth), cols], preferred_element_type=jnp.float32
            )
            for t in range(NTP):
                pst[c, t % 2, t // 2, pl.ds(g * 8, 8), :] = prod[t * 8 : (t + 1) * 8, :].astype(
                    jnp.bfloat16
                )
        c_copy(c).start()

    def to_owners(c):
        pltpu.make_async_copy(pst.at[c, 0], cbuf.at[c], c_recv.at[c]).wait()
        xst[c] = (pst[c, core].astype(jnp.float32) + cbuf[c].astype(jnp.float32)).astype(jnp.bfloat16)
        for d in range(1, NX):
            p_copy(c, d).start()

    project(0)
    for c in range(1, N_COL):
        project(c)
        to_owners(c - 1)
    to_owners(N_COL - 1)

    for c in range(N_COL):
        sums = xst[c, x].astype(jnp.float32)
        for d in range(1, NX):
            source = (x + d) % NX
            pltpu.make_async_copy(xst.at[c, 0], rbuf.at[c, source], p_recv.at[c, source]).wait()
            sums = sums + rbuf[c, source].astype(jnp.float32)
        for g in range(2):
            out_ref[:, pl.ds(c * COL + g * (COL // 2), COL // 2)] = sums[g * 8 : (g + 1) * 8].astype(
                jnp.bfloat16
            )

    for i in range(N_HOME):

        @pl.when(2 * i + home_par != z)
        def _():
            q_copy(i).wait_send()

    for kv in range(2):

        @pl.when(new_target != z)
        def _():
            n_copy(kv).wait_send()

    for copy in kv_first + l_copies + kv_copies:
        copy.wait_send()
    for j in range(N_HOME):

        @pl.when(4 * par + j != z)
        def _():
            for g in range(2):
                for src, dst, send, recv in o_pairs(j, g):
                    remote(src, dst, send, recv, at(y, 4 * par + j)).wait_send()

    for c in range(N_COL):
        c_copy(c).wait_send()
        for d in range(1, NX):
            p_copy(c, d).wait_send()


def on_device(queries, new_keys, new_values, cache_keys, cache_values, lengths, turn_start, out_weight):
    vmem = pl.BlockSpec(memory_space=pltpu.VMEM)
    hbm = pl.BlockSpec(memory_space=pl.ANY)
    bf16, f32, i32 = jnp.bfloat16, jnp.float32, jnp.int32
    dma = pltpu.SemaphoreType.DMA
    return pl.pallas_call(
        kernel,
        out_shape=jax.ShapeDtypeStruct((HOME_ROWS // NTP, OUT), bf16),
        in_specs=[hbm] * 8,
        out_specs=vmem,
        scratch_shapes=[
            pltpu.VMEM((HOME_ROWS, GROUP * HD), bf16),
            pltpu.SMEM((1, 8), i32),
            pltpu.SMEM((8,), i32),
            pltpu.VMEM((QC, HD), bf16),
            pltpu.VMEM((N_HOME, QC, HD), bf16),
            pltpu.VMEM((2 * NY, SHARD, HD), bf16),
            pltpu.VMEM((2 * NY, SHARD, HD), bf16),
            pltpu.VMEM((2 * SHARD, HD), bf16),
            pltpu.VMEM((VROWS, 2 * SHARD), bf16),
            pltpu.VMEM((2 * SHARD, QC), f32),
            pltpu.VMEM((2 * SHARD, QC), f32),
            pltpu.VMEM((NY, 2, 8, 128), i32),
            pltpu.VMEM((NY, 3, 8, 128), i32),
            pltpu.VMEM((HOME_ROWS, HD), bf16),
            pltpu.VMEM((HOME_ROWS, HD), bf16),
            pltpu.VMEM((VROWS, HOME_ROWS), bf16),
            pltpu.VMEM((N_HOME, VROWS, QC), f32),
            pltpu.VMEM((N_HOME, 8, QC), f32),
            pltpu.VMEM((N_HOME, 2, HD, GL), bf16),
            pltpu.VMEM((N_HOME, 2, 8, 128), f32),
            pltpu.VMEM((N_HOME, 2, HD, GL), bf16),
            pltpu.VMEM((N_HOME, 2, 8, 128), f32),
            pltpu.VMEM((2, HOME_ROWS, GROUP * HD // 2), bf16),
            pltpu.VMEM((HOME_ROWS, OUT), f32),
            pltpu.VMEM((GROUP * HD, OUT), bf16),
            pltpu.VMEM((N_COL, 2, NX, 16, COL // 2), bf16),
            pltpu.VMEM((N_COL, NX, 16, COL // 2), bf16),
            pltpu.VMEM((N_COL, NX, 16, COL // 2), bf16),
            pltpu.VMEM((N_COL, NX, 16, COL // 2), bf16),
            dma((3,)),
            dma,
            dma((2 * NY, 2, 2)),
            dma((2 * NY, 2, 2)),
            dma((NY, 3)),
            dma((NY, 3)),
            dma((N_HOME,)),
            dma((N_HOME,)),
            dma((2,)),
            dma((2,)),
            dma((N_HOME, 2)),
            dma((N_HOME, 2)),
            dma((N_HOME, 2)),
            dma((N_HOME, 2)),
            dma((N_COL,)),
            dma((N_COL,)),
            dma((N_COL, NX)),
            dma((N_COL, NX)),
        ],
        compiler_params=pltpu.CompilerParams(
            collective_id=0, has_side_effects=True, vmem_limit_bytes=60 << 20
        ),
        name="attend_project",
    )(queries, new_keys, new_values, cache_keys, cache_values, lengths.T, turn_start, out_weight)


def solution(mesh):
    in_specs = (
        P("ctx", "tp"),
        P("ctx", "tp"),
        P("ctx", "tp"),
        P(None, "ctx", "tp"),
        P(None, "ctx", "tp"),
        P(None, "ctx"),
        P(),
        P("tp", None),
    )
    return jax.shard_map(
        on_device, mesh=mesh, in_specs=in_specs, out_specs=P(("ctx", "tp"), None), check_vma=False
    )
```

time: 92.5 us -> 75.8 us (0.82); the launches traced: 91.9 us -> 74.3 us
  Pallas kernels: 84.7 us -> 72.8 us
  local copies, waits for them, and re-layouts: 7.17 us -> 1.47 us
    pallas_call x1, Pallas kernels: 84.7 us -> 72.8 us  [on_device(): pl.pallas_call(kernel, out_shape=jax.ShapeDtypeStruct((HOME_ROWS // NTP,...]
    unnamed x14 -> x1, local copies, waits for them, and re-layouts: 7.17 us -> 1.47 us
where the time goes in v2:
time: 75.8 us; the launch traced here: 74.3 us
  Pallas kernels  72.8 us (96%)
  local copies, waits for them, and re-layouts  1.47 us (2%)
    pallas_call x1, Pallas kernels, on_device(): pl.pallas_call(kernel, out_shape=jax.ShapeDtypeStruct((HOME_ROWS // NTP,...  72.8 us

profile of v2, /device:TPU:64, one launch (start us, length us, event | category | flops | bytes accessed | tf_op | source)
XLA Modules:
  0.0 74.3 jit_solution(13664051924865054819)
XLA Ops:
  0.0 72.8 %attend_project.1 = bf16[8,4096]{1,0:T(8,128)(2,1)} custom-call(bf16[64,1024]{1,0:T(8,128)(2,1)} %q_hbm.1, bf16[64,128]{1,0:T(8,128)(2,1)} %nk_ref.1, bf16[64,128]{1,0:T(8,128)(2,1)} %nv_ref.1, bf16[8,768,128]{2,1,0:T(8,128)(2,1)} %ck_ref.1, bf16[8,768,128]{2,1,0:T(8,128)(2,1)} %cv_ref.1, s32[1,8]{1,0:T(1,128)} %bitcast.1, s32[8]{0:T(128)} %start_hbm.1, ...), custom_call_target="tpu_custom_call" | custom-call | tf_op jit(solution)/shard_map/attend_project/pallas_call | solution.py:422
  72.8 1.5 %copy.10 = bf16[8,4096]{1,0:T(8,128)(2,1)} copy(bf16[8,4096]{1,0:T(8,128)(2,1)} %attend_project.1) | data formatting | bytes 131072

commit v3 on v2

--- a/solution.py
+++ b/solution.py
@@ -27,6 +27,7 @@
 N_COL = 4
 COL = OUT // N_COL
 MESH = pl.DeviceIdType.MESH
+ORDER = (2, 4, 1, -1, -2, -3, -4, 3, 5, 7, 6)
 
 
 def kernel(
@@ -109,8 +110,7 @@
             device_id=device, device_id_type=MESH,
         )
 
-    kv_first = []
-    kv_copies = []
+    by_block = {}
     l_copies = []
     for oi in range(NY):
         row = row_of(oi)
@@ -136,10 +136,7 @@
                         src.at[traj, rows], dst.at[b, rows],
                         kv_send.at[b, h, kv], kv_recv.at[b, h, kv], device,
                     )
-                    (kv_first if oi in (1, 2) and not cross else kv_copies).append(copy)
-    for copy in kv_first:
-        copy.start()
-
+                    by_block.setdefault(2 * oi + cross, []).append(copy)
     def q_copy(i):
         return remote(
             qst, qbuf.at[home_slot], q_send.at[i], q_recv.at[home_slot], at(y, 2 * i + home_par)
@@ -148,7 +145,7 @@
     def q_local():
         return pltpu.make_async_copy(qst, qbuf.at[home_slot], q_recv.at[home_slot])
 
-    for i in range(N_HOME):
+    def send_queries(i):
         target = 2 * i + home_par
 
         @pl.when(target != z)
@@ -179,15 +176,24 @@
         def _():
             n_local(kv).start()
 
-    for copy in l_copies + kv_copies:
+    for copy in l_copies:
         copy.start()
+
+    for item in ORDER:
+        if item < 0:
+            send_queries(-1 - item)
+        else:
+            for copy in by_block[item]:
+                copy.start()
 
     acc[...] = jnp.zeros_like(acc)
     mx[...] = jnp.full_like(mx, MASKED)
     sst[...] = jnp.zeros_like(sst)
 
-    for j in range(N_HOME):
-        pltpu.make_async_copy(qst, qbuf.at[j], q_recv.at[j]).wait()
+    chunks = list(range(N_HOME))
+
+    def queries_here(k):
+        pltpu.make_async_copy(qst, qbuf.at[chunks[k]], q_recv.at[chunks[k]]).wait()
 
     def scores(keys, j, held_scores):
         s = lax.dot_general(
@@ -205,15 +211,21 @@
         part = jnp.dot(vt_rows, p, preferred_element_type=jnp.float32)
         acc[j] = acc[j] * fade + part
 
-    def sweep(first, count, done=None):
+    def sweep(first, count, ready=None, done=None):
         rows = pl.ds(first, count)
         buffers = (sa.at[pl.ds(0, count)], sb.at[pl.ds(0, count)])
-        state = scores(kp[rows, :], 0, buffers[0])
-        for j in range(N_HOME):
-            ahead = scores(kp[rows, :], j + 1, buffers[(j + 1) % 2]) if j + 1 < N_HOME else None
-            update(j, buffers[j % 2][...], *state, vt[:, rows])
+
+        def begin(k):
+            if ready is not None:
+                ready(k)
+            return scores(kp[rows, :], chunks[k], buffers[k % 2])
+
+        state = begin(0)
+        for k in range(N_HOME):
+            ahead = begin(k + 1) if k + 1 < N_HOME else None
+            update(chunks[k], buffers[k % 2][...], *state, vt[:, rows])
             if done is not None:
-                done(j)
+                done(chunks[k])
             state = ahead
 
     position = lax.broadcasted_iota(jnp.int32, (HALF, HD), 0)
@@ -247,10 +259,10 @@
                     jnp.bfloat16
                 )
 
-    for oi in range(NY - 1):
-        arrive(2 * oi, 0)
-        arrive(2 * oi + 1, SHARD)
-        sweep(0, 2 * SHARD)
+    for first, second in ((0, 1), (2, 4), (3, 5)):
+        arrive(first, 0)
+        arrive(second, SHARD)
+        sweep(0, 2 * SHARD, ready=queries_here if first == 0 else None)
 
     for kv in range(2):
         pltpu.make_async_copy(
@@ -272,9 +284,9 @@
         mx[j, 0:1, :] = new
         update(j, s, old, new, vtn[...])
 
+    arrive(2 * NY - 1, 0)
+    sweep(0, SHARD)
     arrive(2 * NY - 2, 0)
-    sweep(0, SHARD)
-    arrive(2 * NY - 1, 0)
 
     def o_pairs(j, g):
         me = z // 2
@@ -300,8 +312,8 @@
             for src, dst, send, recv in o_pairs(j, g):
                 pltpu.make_async_copy(src, dst, recv).start()
 
-    sweep(0, SHARD, lambda j: send_partial(j, 0))
-    for j in range(N_HOME):
+    sweep(0, SHARD, done=lambda j: send_partial(j, 0))
+    for j in chunks:
         send_partial(j, 1)
 
     w_copy.wait()
@@ -398,7 +410,7 @@
         def _():
             n_copy(kv).wait_send()
 
-    for copy in kv_first + l_copies + kv_copies:
+    for copy in l_copies + [copy for block in by_block.values() for copy in block]:
         copy.wait_send()
     for j in range(N_HOME):
 

time: 75.8 us -> 75.4 us (level); the launches traced: 74.3 us -> 75.3 us
  Pallas kernels: 72.8 us -> 73.8 us
    pallas_call x1, Pallas kernels: 72.8 us -> 73.8 us  [on_device(): pl.pallas_call(kernel, out_shape=jax.ShapeDtypeStruct((HOME_ROWS // NTP,...]
where the time goes in v3:
time: 75.4 us; the launch traced here: 75.3 us
  Pallas kernels  73.8 us (98%)
  local copies, waits for them, and re-layouts  1.47 us (2%)
    pallas_call x1, Pallas kernels, on_device(): pl.pallas_call(kernel, out_shape=jax.ShapeDtypeStruct((HOME_ROWS // NTP,...  73.8 us

profile of v3, /device:TPU:64, one launch (start us, length us, event | category | flops | bytes accessed | tf_op | source)
XLA Modules:
  0.0 75.3 jit_solution(8059627867826417141)
XLA Ops:
  0.0 73.8 %attend_project.1 = bf16[8,4096]{1,0:T(8,128)(2,1)} custom-call(bf16[64,1024]{1,0:T(8,128)(2,1)} %q_hbm.1, bf16[64,128]{1,0:T(8,128)(2,1)} %nk_ref.1, bf16[64,128]{1,0:T(8,128)(2,1)} %nv_ref.1, bf16[8,768,128]{2,1,0:T(8,128)(2,1)} %ck_ref.1, bf16[8,768,128]{2,1,0:T(8,128)(2,1)} %cv_ref.1, s32[1,8]{1,0:T(1,128)} %bitcast.1, s32[8]{0:T(128)} %start_hbm.1, ...), custom_call_target="tpu_custom_call" | custom-call | tf_op jit(solution)/shard_map/attend_project/pallas_call | solution.py:434
  73.8 1.5 %copy.10 = bf16[8,4096]{1,0:T(8,128)(2,1)} copy(bf16[8,4096]{1,0:T(8,128)(2,1)} %attend_project.1) | data formatting | bytes 131072

commit v4 on v3

--- a/solution.py
+++ b/solution.py
@@ -27,7 +27,7 @@
 N_COL = 4
 COL = OUT // N_COL
 MESH = pl.DeviceIdType.MESH
-ORDER = (2, 4, 1, -1, -2, -3, -4, 3, 5, 7, 6)
+ORDER = (2, 4, -1, -2, -3, -4, 1, 3, 5, 6, 7)
 
 
 def kernel(
@@ -259,10 +259,10 @@
                     jnp.bfloat16
                 )
 
-    for first, second in ((0, 1), (2, 4), (3, 5)):
-        arrive(first, 0)
-        arrive(second, SHARD)
-        sweep(0, 2 * SHARD, ready=queries_here if first == 0 else None)
+    for oi in range(NY - 1):
+        arrive(2 * oi, 0)
+        arrive(2 * oi + 1, SHARD)
+        sweep(0, 2 * SHARD, ready=queries_here if oi == 0 else None)
 
     for kv in range(2):
         pltpu.make_async_copy(
@@ -284,9 +284,9 @@
         mx[j, 0:1, :] = new
         update(j, s, old, new, vtn[...])
 
+    arrive(2 * NY - 2, 0)
+    sweep(0, SHARD)
     arrive(2 * NY - 1, 0)
-    sweep(0, SHARD)
-    arrive(2 * NY - 2, 0)
 
     def o_pairs(j, g):
         me = z // 2

time: 75.4 us -> 75 us (level)
  no operation moved by 1% of the time
where the time goes in v4:
time: 75 us; the launch traced here: 74.5 us
  Pallas kernels  73.1 us (97%)
  local copies, waits for them, and re-layouts  1.47 us (2%)
    pallas_call x1, Pallas kernels, on_device(): pl.pallas_call(kernel, out_shape=jax.ShapeDtypeStruct((HOME_ROWS // NTP,...  73.1 us

profile of v4, /device:TPU:64, one launch (start us, length us, event | category | flops | bytes accessed | tf_op | source)
XLA Modules:
  0.0 74.5 jit_solution(2511772821214451551)
XLA Ops:
  0.0 73.1 %attend_project.1 = bf16[8,4096]{1,0:T(8,128)(2,1)} custom-call(bf16[64,1024]{1,0:T(8,128)(2,1)} %q_hbm.1, bf16[64,128]{1,0:T(8,128)(2,1)} %nk_ref.1, bf16[64,128]{1,0:T(8,128)(2,1)} %nv_ref.1, bf16[8,768,128]{2,1,0:T(8,128)(2,1)} %ck_ref.1, bf16[8,768,128]{2,1,0:T(8,128)(2,1)} %cv_ref.1, s32[1,8]{1,0:T(1,128)} %bitcast.1, s32[8]{0:T(128)} %start_hbm.1, ...), custom_call_target="tpu_custom_call" | custom-call | tf_op jit(solution)/shard_map/attend_project/pallas_call | solution.py:434
  73.1 1.5 %copy.10 = bf16[8,4096]{1,0:T(8,128)(2,1)} copy(bf16[8,4096]{1,0:T(8,128)(2,1)} %attend_project.1) | data formatting | bytes 131072
